TPU v7x, 256 devices: a whole 4x4x8 slice. The times are simulated.
256 devices in a mesh: section: 64 (over y_hi, x, z), dp: 4 (over y_lo, core).
Axes of the slice: x: 4, y: 4 (y_hi: 2, y_lo: 2; y = y_hi * 2 + y_lo), z: 8, core: 2. Of those that a mesh axis runs over, the one named last changes fastest.
Arguments:
- states: bfloat16 [64, 16, 32, 2688], P('section', None, 'dp'), may hold values from -6 to 6
- inject: bfloat16 [16, 32, 2688], P(None, 'dp'), may hold values from -6 to 6
- final_cotangent: bfloat16 [16, 32, 2688], P(None, 'dp'), may hold values from -6 to 6
- weight: bfloat16 [2688, 2688], P('dp'), may hold values from -0.125 to 0.125
- norm_gain: float32 [2688], replicated, may hold values from 0.1 to 1.9
Outputs:
- d_inject: float32 [16, 32, 2688], P(None, 'dp', 'section')
- d_weight: float32 [2688, 2688], P('section', 'dp')
- d_gain: float32 [2688], replicated
All inputs are finite; a program needn't handle non-finite values.
Results may differ from a plain program's by a relative error of at most 0.018.
Values may be sent and summed in bfloat16 or wider, within the bound.
No kernel may reach another device: no remote copies, remote signals or barrier semaphores. Data moves between devices by JAX's collectives and lax.ppermute only.
A program may use at most 128 MiB of HBM per device.

v0:
```python
import functools
import math

import jax
import jax.numpy as jnp
from jax import lax
from jax.experimental import pallas as pl
from jax.experimental.pallas import tpu as pltpu
from jax.sharding import PartitionSpec as P

EPSILON = 1e-06
TOLERANCE = 2.0**-10
LANES = 128
WIDE = 512
AXES = ("section", "dp")
Y_HI, X, Z, Y_LO, CORE = 2, 4, 8, 2, 2
f32, bf16 = jnp.float32, jnp.bfloat16


def own_tokens(ref, section, copies):
    block = ref[section // 4].astype(f32)
    pair = block[0:2]
    for k in range(1, 4):
        pair = jnp.where(section % 4 == k, block[2 * k : 2 * k + 2], pair)
    return jnp.concatenate([pair] * copies, axis=0)


def prepare_kernel(place_ref, states_ref, inject_ref, gain_ref, x_ref, a_ref, q_ref, *cut_refs):
    rows, dim = x_ref.shape
    section = place_ref[0]
    inject = own_tokens(inject_ref, section, 4)
    gain = gain_ref[...]
    groups = rows // 8

    def one(b, _):
        x = jnp.concatenate([states_ref[seg * groups + b].astype(f32) for seg in range(4)], axis=0) + inject
        q = lax.rsqrt(jnp.sum(x * x, axis=1, keepdims=True) * (1.0 / dim) + EPSILON)
        at = pl.ds(pl.multiple_of(b * 8, 8), 8)
        x_ref[at, :] = x
        q_ref[at, :] = jnp.broadcast_to(q, (8, LANES))
        return 0

    lax.fori_loop(0, groups, one, 0)
    a_ref[...] = (x_ref[...] * q_ref[:, 0:1] * gain).astype(bf16)
    eighth = dim // 8
    place = (section // Z) % X
    for cut_ref in cut_refs:
        cut_ref[:, 2 * eighth :] = jnp.zeros((rows, cut_ref.shape[1] - 2 * eighth), bf16)
    for own in range(X):

        @pl.when(place == own)
        def _():
            for step in range(X):
                k = (own + step) % X
                cut_refs[step][:, 0:eighth] = a_ref[:, k * eighth : (k + 1) * eighth]
                cut_refs[step][:, eighth : 2 * eighth] = a_ref[:, dim // 2 + k * eighth : dim // 2 + (k + 1) * eighth]


def prepare(place, states, inject, gain):
    rows, dim = states.shape[0] * states.shape[1], states.shape[2]
    vm = pl.BlockSpec(memory_space=pltpu.VMEM)
    return pl.pallas_call(
        prepare_kernel,
        out_shape=(
            jax.ShapeDtypeStruct((rows, dim), f32),
            jax.ShapeDtypeStruct((rows, dim), bf16),
            jax.ShapeDtypeStruct((rows, LANES), f32),
        )
        + (jax.ShapeDtypeStruct((rows, pl.cdiv(dim // 4, LANES) * LANES), bf16),) * X,
        in_specs=[pl.BlockSpec(memory_space=pltpu.SMEM)] + [vm] * 3,
        out_specs=(vm,) * (3 + X),
        compiler_params=pltpu.CompilerParams(vmem_limit_bytes=32 * 2**20),
        cost_estimate=pl.CostEstimate(flops=20 * 10**9, bytes_accessed=4 * 2**20, transcendentals=0),
    )(place, states, inject, gain)


def solve_kernel(offsets, max_sweeps, tolerance, place_ref, *refs):
    count = len(offsets)
    pieces = refs[:count]
    a_ref, x_ref, q_ref, gain_ref, final_ref = refs[count : count + 5]
    outs = refs[count + 5 : count + 9]
    w, wt, slope, t, p, v, inject_sum, gain_sum, final, sems = refs[count + 9 :]
    rows, dim = x_ref.shape
    section, shard = place_ref[0], place_ref[1]
    small, eighth, groups = dim // 4, dim // 8, rows // 8

    blocks = [(low, min(WIDE, dim - low)) for low in range(0, dim, WIDE)]
    copies = {}
    for m, (low, width) in enumerate(blocks):
        for n, ((flip, start, length), piece) in enumerate(zip(offsets, pieces)):
            at = pl.multiple_of(lax.bitwise_xor(shard, flip) * small + start, 16)
            copies[m, n] = pltpu.make_async_copy(
                piece.at[:, pl.ds(low, width)], w.at[pl.ds(at, length), pl.ds(low, width)], sems.at[m, n]
            )
            copies[m, n].start()
    final[...] = own_tokens(final_ref, section, 4)
    p[...] = jnp.zeros_like(p)
    for m, (low, width) in enumerate(blocks):
        for n in range(count):
            copies[m, n].wait()
        cols = slice(low, low + width)
        h = jnp.dot(a_ref[...], w[:, cols], preferred_element_type=f32)
        s = jax.nn.sigmoid(h)
        sl = s * (1.0 + h * (1.0 - s)) * (1.0 / math.sqrt(max_sweeps))
        slope[:, cols] = sl
        v[:, cols] = (sl * jnp.concatenate([final[:, cols]] * groups, axis=0)).astype(bf16)
        wt[cols, :] = w[:, cols].T
    sub = lax.broadcasted_iota(jnp.int32, (8, LANES), 0)

    def sweep(carry):
        done, _ = carry
        acc = jnp.zeros((rows, LANES), f32)
        for j, width in blocks:
            cols = slice(j, j + width)
            u = jnp.dot(v[...], wt[:, cols], preferred_element_type=f32)
            scaled = u * gain_ref[0:1, cols]
            t[:, cols] = scaled
            scaled = scaled * x_ref[:, cols]
            for k in range(0, width, LANES):
                acc = acc + scaled[:, k : k + LANES]
        q = q_ref[...]
        kappa = q * q * q * (jnp.sum(acc, axis=1, keepdims=True) * (1.0 / dim))

        def columns(n, sums):
            moved, size = sums
            cols = pl.ds(pl.multiple_of(n * LANES, LANES), LANES)
            run, tails = None, [None] * groups
            for b in range(groups - 1, -1, -1):
                at = slice(8 * b, 8 * b + 8)
                new = q[at] * t[at, cols] - kappa[at] * x_ref[at, cols]
                step = new - p[at, cols]
                p[at, cols] = new
                moved = moved + step * step
                run = new if run is None else run + new
                tails[b] = run
            inject_sum[:, cols] = run
            base = final[:, cols]
            for k in (2, 4, 6):
                base = base + jnp.where(sub < 8 - k, pltpu.roll(run, 8 - k, 0), 0.0)
            for b in range(groups):
                at = slice(8 * b, 8 * b + 8)
                c = base if b == groups - 1 else base + tails[b + 1]
                size = size + c * c
                v[at, cols] = (c * slope[at, cols]).astype(bf16)
            return moved, size

        zero = jnp.zeros((8, LANES), f32)
        moved, size = lax.fori_loop(0, dim // LANES, columns, (zero, zero), unroll=3)
        moved = jnp.sum(moved, axis=1, keepdims=True)
        size = jnp.sum(size, axis=1, keepdims=True)
        still = jnp.sum(jnp.where(moved <= size * (tolerance * tolerance), 0.0, 1.0))
        return done + 1, still

    lax.while_loop(
        lambda carry: jnp.logical_and(carry[0] < max_sweeps, carry[1] > 0.0),
        sweep,
        (jnp.int32(0), jnp.float32(1)),
    )

    def finish(n, _):
        cols = pl.ds(pl.multiple_of(n * LANES, LANES), LANES)
        acc = jnp.zeros((8, LANES), f32)
        for b in range(groups):
            at = slice(8 * b, 8 * b + 8)
            acc = acc + q_ref[at] * t[at, cols] * x_ref[at, cols]
        gain_sum[:, cols] = acc / gain_ref[0:1, cols]
        return 0

    lax.fori_loop(0, dim // LANES, finish, 0)
    wide_sub = lax.broadcasted_iota(jnp.int32, (8, small), 0)
    gain_rows = jnp.zeros((8, small), f32)
    total = jnp.sum(gain_sum[...], axis=0, keepdims=True)
    for k in range(4):
        gain_rows = jnp.where(wide_sub == k, total[:, k * small : (k + 1) * small], gain_rows)
    inject_rows = jnp.zeros((8, small), f32)
    total = inject_sum[...]
    total = total + pltpu.roll(total, 4, 0)
    total = total + pltpu.roll(total, 2, 0)
    for k in range(X):
        part = jnp.concatenate(
            [total[:, k * eighth : (k + 1) * eighth], total[:, dim // 2 + k * eighth : dim // 2 + (k + 1) * eighth]],
            axis=1,
        )
        inject_rows = jnp.where(wide_sub // 2 == k, part, inject_rows)
    extra = jnp.concatenate([inject_rows, gain_rows], axis=0).astype(bf16)
    for own in range(4):

        @pl.when(shard == own)
        def _():
            for flip in range(4):
                block = own ^ flip
                outs[flip][0:rows] = v[:, block * small : (block + 1) * small]

    for flip in range(4):
        outs[flip][rows : rows + 16] = extra


def solve(place, pieces, offsets, a, x, q, gain, final, tolerance):
    rows, dim = x.shape
    n = len(pieces)
    vm = pl.BlockSpec(memory_space=pltpu.VMEM)
    return pl.pallas_call(
        functools.partial(solve_kernel, offsets, 64, tolerance),
        out_shape=(jax.ShapeDtypeStruct((rows + 16, dim // 4), bf16),) * 4,
        in_specs=[pl.BlockSpec(memory_space=pltpu.SMEM)] + [pl.BlockSpec(memory_space=pl.ANY)] * n + [vm] * 5,
        out_specs=(vm,) * 4,
        scratch_shapes=[pltpu.VMEM((dim, dim), bf16)] * 2
        + [pltpu.VMEM((rows, dim), f32)] * 3
        + [pltpu.VMEM((rows, dim), bf16)]
        + [pltpu.VMEM((8, dim), f32)] * 3
        + [pltpu.SemaphoreType.DMA((pl.cdiv(dim, WIDE), n))],
        compiler_params=pltpu.CompilerParams(vmem_limit_bytes=56 * 2**20),
        cost_estimate=pl.CostEstimate(flops=4 * 10**10, bytes_accessed=16 * 2**20, transcendentals=0),
    )(place, *pieces, a, x, q, gain, final)


def block_kernel(rows, dim, place_ref, *refs):
    a_refs, own_refs, far_refs = refs[:4], refs[4:8], refs[8:12]
    out_ref, a, g, sems = refs[12:]
    small, part = dim // 4, dim // 64
    tall = rows + 16
    copies = [pltpu.make_async_copy(a_refs[flip], a.at[flip], sems.at[flip]) for flip in range(4)]
    for step in range(X):
        copies.append(pltpu.make_async_copy(own_refs[step], g.at[pl.ds(step * tall, tall)], sems.at[4 + step]))
        copies.append(pltpu.make_async_copy(far_refs[step], g.at[pl.ds((4 + 3 * step) * tall, 3 * tall)], sems.at[8 + step]))
    for copy in copies:
        copy.start()
    for copy in copies:
        copy.wait()

    def slot(flip, step):
        return tall * (step if flip == 0 else 3 + 3 * step + flip)

    places = [(flip, step) for flip in range(4) for step in range(X)]
    left = jnp.concatenate([a[flip, step * rows : (step + 1) * rows] for flip, step in places], axis=0)
    right = jnp.concatenate([g[slot(flip, step) : slot(flip, step) + rows] for flip, step in places], axis=0)
    block = lax.dot_general(left, right, (((0,), (0,)), ((), ())), preferred_element_type=f32)
    gain = jnp.zeros((8, small), f32)
    injects = []
    for flip, step in places:
        extra = g[slot(flip, step) + rows : slot(flip, step) + tall].astype(f32)
        gain = gain + extra[8:16]
        if flip == 0:
            own = extra[0:2]
            for k in range(1, X):
                own = jnp.where((place_ref[0] // Z) % X == k, extra[2 * k : 2 * k + 2], own)
            injects.append(own)
    inject = jnp.concatenate(injects, axis=0)
    for k in range(16):
        line = jnp.concatenate(
            [inject[n : n + 1, k * part : (k + 1) * part] for n in range(8)] + [jnp.zeros((1, small - 8 * part), f32)],
            axis=1,
        )
        out_ref[k] = jnp.concatenate([block[k * part : (k + 1) * part], line, gain[0:5]], axis=0).astype(bf16)


def block_sum(place, a_parts, own_parts, far_parts):
    rows, small = a_parts[0].shape[0] // X, own_parts[0].shape[1]
    hold = pl.BlockSpec(memory_space=pl.ANY)
    return pl.pallas_call(
        functools.partial(block_kernel, rows, 4 * small),
        out_shape=jax.ShapeDtypeStruct((16, 48, small), bf16),
        in_specs=[pl.BlockSpec(memory_space=pltpu.SMEM)] + [hold] * 12,
        out_specs=pl.BlockSpec(memory_space=pltpu.VMEM),
        scratch_shapes=[
            pltpu.VMEM((4,) + a_parts[0].shape, bf16),
            pltpu.VMEM((16 * (rows + 16), small), bf16),
            pltpu.SemaphoreType.DMA((12,)),
        ],
        compiler_params=pltpu.CompilerParams(vmem_limit_bytes=48 * 2**20),
    )(place, *a_parts, *own_parts, *far_parts)


def flat(y, x, z, core):
    return (((y // Y_LO) * X + x) * Z + z) * 4 + (y % Y_LO) * CORE + core


PLACES = [
    (y, x, z, core)
    for y in range(Y_HI * Y_LO)
    for x in range(X)
    for z in range(Z)
    for core in range(CORE)
]


def move(value, target):
    return lax.ppermute(value, AXES, [(flat(*place), flat(*target(*place))) for place in PLACES])


def y_move(value, steps):
    return move(value, lambda y, x, z, core: ((y + steps) % (Y_HI * Y_LO), x, z, core))


def x_move(value, steps):
    return move(value, lambda y, x, z, core: (y, (x + steps) % X, z, core))


def dp_move(value, flip):
    return move(value, lambda y, x, z, core: (y ^ (flip // CORE), x, z, core ^ (flip % CORE)))


YZ_GROUPS = [
    [flat(yh * Y_LO + d // CORE, x, z, d % CORE) for yh in range(Y_HI) for z in range(Z)]
    for x in range(X)
    for d in range(4)
]


def fetch_weight(weight):
    half = weight.shape[0] // 2
    cuts = (0, 128, 336)
    source, landed = weight, []
    for low, high in zip(cuts[:-1], cuts[1:]):
        up, down = y_move(source[low:high], 1), y_move(source[half + low : half + high], -1)
        source, up, down = lax.optimization_barrier((source, up, down))
        landed += [(low, up), (half + low, down)]
    return landed


def share_weight(weight, landed):
    pieces, offsets = [weight, dp_move(weight, 1)], [(0, 0, weight.shape[0]), (1, 0, weight.shape[0])]
    for start, piece in landed:
        pieces += [piece, dp_move(piece, 1)]
        offsets += [(2, start, piece.shape[0]), (3, start, piece.shape[0])]
    return pieces, tuple(offsets)


def per_device(states, inject, final_cotangent, weight, norm_gain):
    micro_count, row_count, dim = inject.shape
    sections = lax.axis_size("section")
    section, shard = lax.axis_index("section"), lax.axis_index("dp")
    own = micro_count * row_count // sections
    place = jnp.stack([section, shard]).astype(jnp.int32)
    gain = norm_gain.reshape(1, dim)
    landed = fetch_weight(weight)

    mine = lax.all_to_all(states[0].reshape(sections, own, dim), "section", 0, 0)
    x, a, q, *a_cut = prepare(place, mine, inject, gain)

    a_ring = jnp.concatenate([a_cut[0]] + [x_move(a_cut[step], step) for step in range(1, X)])
    (low, up), (high, down) = landed[-2:]
    up, down, a_ring = lax.optimization_barrier((up, down, a_ring))
    landed[-2:] = [(low, up), (high, down)]
    pieces, offsets = share_weight(weight, landed)
    a_parts = [a_ring] + [dp_move(a_ring, flip) for flip in (1, 2, 3)]

    g_parts = solve(place, pieces, offsets, a, x, q, gain, final_cotangent, TOLERANCE)

    (a_parts, g_parts) = lax.optimization_barrier((a_parts, g_parts))
    far = jnp.concatenate([dp_move(g_parts[flip], flip) for flip in (1, 2, 3)])
    own_parts = [g_parts[0]] + [x_move(g_parts[0], step) for step in range(1, X)]
    far, own_parts = lax.optimization_barrier((far, own_parts))
    far_parts = [far] + [x_move(far, step) for step in range(1, X)]
    out = block_sum(place, a_parts, own_parts, far_parts)

    got = lax.all_to_all(out, AXES, 0, 0, axis_index_groups=YZ_GROUPS)
    part = dim // 64
    total = jnp.sum(got.astype(f32), axis=0)
    d_weight = total[:part]
    d_gain = total[part + 1 : part + 5].reshape(dim)
    d_inject = got[:, part, : X * own * part].reshape(Y_HI, Z, X, own, part)
    d_inject = jnp.roll(d_inject[:, :, ::-1], (section // Z) % X + 1, axis=2).transpose(0, 2, 1, 3, 4)
    d_inject = d_inject.reshape(micro_count, row_count, part).astype(f32)
    return d_inject, d_weight, d_gain


def solution(mesh):
    in_specs = (
        P("section", None, "dp", None),
        P(None, "dp", None),
        P(None, "dp", None),
        P("dp", None),
        P(),
    )
    out_specs = (P(None, "dp", "section"), P("section", "dp"), P())
    return jax.shard_map(
        per_device, mesh=mesh, in_specs=in_specs, out_specs=out_specs, check_vma=False
    )
```

profile of v0, /device:TPU:8, one launch (start us, length us, event | category | flops | bytes accessed | tf_op | source)
XLA Modules:
  0.0 218.0 jit_solution(4792489680136084577)
XLA Ops:
  0.6 1.5 fusion.2
  2.1 1.7 collective-permute-start
  3.8 0.7 collective-permute-start.1
  4.5 1.1 reshape_squeeze.6
  5.6 13.4 %all-to-all-start = ((bf16[64,2,2688]{2,1,0:T(2,128)(2,1)}), bf16[64,2,2688]{2,1,0:T(2,128)(2,1)S(1)}, u32[]{:S(2)}, u32[]{:S(2)}) async-start(bf16[64,2,2688]{2,1,0:T(2,128)(2,1)} %reshape_squeeze.6), calls=%async_computation | async-start | bytes 1376256 | tf_op jit(solution)/shard_map/all_to_all | solution.py:338
  19.4 1.4 collective-permute-done.1.refs_4_
  20.8 2.8 %fusion.1 = (bf16[208,2688]{1,0:T(8,128)(2,1)S(1)}, bf16[208,2688]{1,0:T(8,128)(2,1)}) fusion(bf16[672,2688]{1,0:T(8,128)(2,1)} %refs_0_.1), kind=kLoop, calls=%fused_computation.9 | loop fusion | bytes 4472832 | tf_op jit(solution)/shard_map/slice | solution.py:315
  23.6 1.4 collective-permute-start.2
  25.0 0.6 collective-permute-start.3
  25.6 15.9 %all-to-all-done.states_ref = bf16[64,2,2688]{2,1,0:T(2,128)(2,1)S(1)} async-done(((bf16[64,2,2688]{2,1,0:T(2,128)(2,1)}), bf16[64,2,2688]{2,1,0:T(2,128)(2,1)S(1)}, u32[]{:S(2)}, u32[]{:S(2)}) %all-to-all-start) | async-done | bytes 688160 | tf_op jit(solution)/shard_map/all_to_all | solution.py:338
  41.6 3.1 %shard_map.76 = (f32[128,2688]{1,0:T(8,128)S(1)}, bf16[128,2688]{1,0:T(8,128)(2,1)S(1)}, f32[128,128]{1,0:T(8,128)S(1)}, bf16[128,768]{1,0:T(8,128)(2,1)S(1)}, b...) custom-call(s32[2]{0:T(128)S(1)} %pad_add_fusion.place_ref, ...), custom_call_target="tpu_custom_call" | custom-call | flops 20000000000 | bytes 4194304 | tf_op jit(solution)/shard_map/pallas_call | solution.py:62
  44.7 0.8 copy-done.6
  45.6 4.2 %collective-permute-start.5 = (bf16[128,768]{1,0:T(8,128)(2,1)S(1)}, bf16[128,768]{1,0:T(8,128)(2,1)S(1)}, u32[]{:S(2)}, u32[]{:S(2)}) collective-permute-start(bf16[128,768]{1,0:T(8,128)(2,1)S(1)} %get-tuple-element.40), channel_id=1, source_target_pairs={{0,64},{1,65},{4,68},{5,69},{8,72},{9,73},{12,76},{13,77},{16,80},... | collective-permute-start | bytes 589832 | tf_op jit(solution)/shard_map/ppermute | solution.py:288
  49.8 3.8 %collective-permute-done.4 = bf16[128,768]{1,0:T(8,128)(2,1)S(1)} collective-permute-done((bf16[128,768]{1,0:T(8,128)(2,1)S(1)}, bf16[128,768]{1,0:T(8,128)(2,1)S(1)}, u32[]{:S(2)}, u32[]{:S(2)}) %collective-permute-start.4) | collective-permute-done | bytes 196640 | tf_op jit(solution)/shard_map/ppermute | solution.py:288
  53.6 0.6 collective-permute-start.6
  54.2 1.5 collective-permute-done.5
  55.7 3.6 %collective-permute-done.6 = bf16[128,768]{1,0:T(8,128)(2,1)S(1)} collective-permute-done((bf16[128,768]{1,0:T(8,128)(2,1)S(1)}, bf16[128,768]{1,0:T(8,128)(2,1)S(1)}, u32[]{:S(2)}, u32[]{:S(2)}) %collective-permute-start.6) | collective-permute-done | bytes 196640 | tf_op jit(solution)/shard_map/ppermute | solution.py:288
  59.5 0.5 collective-permute-start.14
  60.1 0.4 collective-permute-start.12
  60.5 3.7 %collective-permute-done.11.refs_3_ = bf16[128,2688]{1,0:T(8,128)(2,1)S(1)} collective-permute-done((bf16[128,2688]{1,0:T(8,128)(2,1)S(1)}, bf16[128,2688]{1,0:T(8,128)(2,1)S(1)}, u32[]{:S(2)}, u32[]{:S(2)}) %collective-permute-start.11) | collective-permute-done | bytes 688160 | tf_op jit(solution)/shard_map/ppermute | solution.py:288
  64.2 0.1 collective-permute-start.7
  64.3 1.7 collective-permute-done.12.refs_5_
  66.0 1.3 collective-permute-start.8
  67.4 0.4 collective-permute-start.9
  67.8 0.7 copy-done.12
  68.5 0.3 copy-done.13
  68.8 47.0 %shard_map.77 = (bf16[144,672]{1,0:T(8,128)(2,1)}, bf16[144,672]{1,0:T(8,128)(2,1)}, bf16[144,672]{1,0:T(8,128)(2,1)}, bf16[144,672]{1,0:T(8,128)(2,1)}) custom-call(s32[2]{0:T(128)} %copy-done.2, bf16[672,2688]{1,0:T(8,128)(2,1)} %refs_0_.1, bf16[672,2688]{1,0:T(8,128)(2,1)} %collective-permute-done.10.refs_1_, bf16[128,2688]{1,0:T(8,128)(2,1)} %copy-done.14, ...), custom_call_target="tpu_custom_call" | custom-call | flops 40000000000 | bytes 16777216 | tf_op jit(solution)/shard_map/pallas_call | solution.py:202
  115.8 4.0 %collective-permute-start.15 = (bf16[144,672]{1,0:T(8,128)(2,1)}, bf16[144,672]{1,0:T(8,128)(2,1)S(1)}, u32[]{:S(2)}, u32[]{:S(2)}) collective-permute-start(bf16[144,672]{1,0:T(8,128)(2,1)} %get-tuple-element.58), channel_id=1, source_target_pairs={{0,1},{1,0},{4,5},{5,4},{8,9},{9,8},{12,13},{13,12},{16,17},{17,16... | collective-permute-start | bytes 580616 | tf_op jit(solution)/shard_map/ppermute | solution.py:288
  119.9 1.4 collective-permute-start.17
  121.3 1.5 collective-permute-start.18
  122.8 1.7 collective-permute-start.19
  124.5 1.0 collective-permute-start.20
  125.5 2.8 %collective-permute-done.16 = bf16[144,672]{1,0:T(8,128)(2,1)S(1)} collective-permute-done((bf16[144,672]{1,0:T(8,128)(2,1)}, bf16[144,672]{1,0:T(8,128)(2,1)S(1)}, u32[]{:S(2)}, u32[]{:S(2)}) %collective-permute-start.16) | collective-permute-done | bytes 193568 | tf_op jit(solution)/shard_map/ppermute | solution.py:288
  128.3 3.0 %collective-permute-done.17 = bf16[144,672]{1,0:T(8,128)(2,1)S(1)} collective-permute-done((bf16[144,672]{1,0:T(8,128)(2,1)}, bf16[144,672]{1,0:T(8,128)(2,1)S(1)}, u32[]{:S(2)}, u32[]{:S(2)}) %collective-permute-start.17) | collective-permute-done | bytes 193568 | tf_op jit(solution)/shard_map/ppermute | solution.py:288
  131.5 4.0 %collective-permute-done.19.refs_6_ = bf16[144,672]{1,0:T(8,128)(2,1)S(1)} collective-permute-done((bf16[144,672]{1,0:T(8,128)(2,1)}, bf16[144,672]{1,0:T(8,128)(2,1)S(1)}, u32[]{:S(2)}, u32[]{:S(2)}) %collective-permute-start.19) | collective-permute-done | bytes 193568 | tf_op jit(solution)/shard_map/ppermute | solution.py:288
  135.5 0.6 collective-permute-done.20.refs_7_
  136.1 1.2 collective-permute-start.21
  137.3 2.9 %collective-permute-start.22 = (bf16[432,672]{1,0:T(8,128)(2,1)S(1)}, bf16[432,672]{1,0:T(8,128)(2,1)S(1)}, u32[]{:S(2)}, u32[]{:S(2)}) collective-permute-start(bf16[432,672]{1,0:T(8,128)(2,1)S(1)} %pad_maximum_fusion.1.refs_8_), channel_id=1, source_target_pairs={{0,64},{1,65},{4,68},{5,69},{8,72},{9,73},{12,76},{13,77},{16,80},... | collective-permute-start | bytes 1741832 | tf_op jit(solution)/shard_map/ppermute | solution.py:288
  140.2 0.4 collective-permute-start.23
  140.6 13.3 %collective-permute-done.21.refs_9_ = bf16[432,672]{1,0:T(8,128)(2,1)S(1)} collective-permute-done((bf16[432,672]{1,0:T(8,128)(2,1)S(1)}, bf16[432,672]{1,0:T(8,128)(2,1)S(1)}, u32[]{:S(2)}, u32[]{:S(2)}) %collective-permute-start.21) | collective-permute-done | bytes 580640 | tf_op jit(solution)/shard_map/ppermute | solution.py:288
  153.9 15.4 %collective-permute-done.22.refs_10_ = bf16[432,672]{1,0:T(8,128)(2,1)S(1)} collective-permute-done((bf16[432,672]{1,0:T(8,128)(2,1)S(1)}, bf16[432,672]{1,0:T(8,128)(2,1)S(1)}, u32[]{:S(2)}, u32[]{:S(2)}) %collective-permute-start.22) | collective-permute-done | bytes 580640 | tf_op jit(solution)/shard_map/ppermute | solution.py:288
  169.3 6.5 %shard_map.78 = bf16[16,48,672]{2,1,0:T(8,128)(2,1)} custom-call(s32[2]{0:T(128)S(1)} %copy-done.3, bf16[512,768]{1,0:T(8,128)(2,1)S(1)} %pad_maximum_fusion.refs_0_, bf16[512,768]{1,0:T(8,128)(2,1)S(1)} %collective-permute-done.7.refs_1_, bf16[512,768]{1,0:T(8,128)(2,1)S(1)} %collective-permute-done.8.refs_2_, bf16[512,768]{1,0:T(8,128)(2,1)} %copy-done.8, ...), custom_call_target="tpu_custom_call" | custom-call | tf_op jit(solution)/shard_map/pallas_call | solution.py:260
  175.8 11.1 %all-to-all-start.1 = ((bf16[16,48,672]{2,1,0:T(8,128)(2,1)}), bf16[16,48,672]{2,1,0:T(8,128)(2,1)S(1)}, u32[]{:S(2)}, u32[]{:S(2)}) async-start(bf16[16,48,672]{2,1,0:T(8,128)(2,1)} %shard_map.78), calls=%async_computation.1 | async-start | bytes 2359296 | tf_op jit(solution)/shard_map/all_to_all | solution.py:357
  186.9 29.2 %all-to-all-done.1 = bf16[16,48,672]{2,1,0:T(8,128)(2,1)S(1)} async-done(((bf16[16,48,672]{2,1,0:T(8,128)(2,1)}), bf16[16,48,672]{2,1,0:T(8,128)(2,1)S(1)}, u32[]{:S(2)}, u32[]{:S(2)}) %all-to-all-start.1) | async-done | bytes 1032224 | tf_op jit(solution)/shard_map/all_to_all | solution.py:357
  216.4 0.1 convert_bitcast_fusion
  216.5 0.7 copy.9
  217.2 0.2 convert_reduce_fusion
  217.3 0.7 reshape.16
  (56 shorter events, 0.9 us)
Async XLA Ops:
  0.6 3.9 %copy-start.9 = (bf16[1,16,8,2688]{3,2,1,0:T(8,128)(2,1)S(1)}, bf16[1,16,8,2688]{3,2,1,0:T(8,128)(2,1)}, u32[]{:S(2)}) copy-start(bf16[1,16,8,2688]{3,2,1,0:T(8,128)(2,1)} %param.5) | copy-start | bytes 2064388
  2.1 17.3 %collective-permute-start = (bf16[128,2688]{1,0:T(8,128)(2,1)S(1)}, bf16[128,2688]{1,0:T(8,128)(2,1)S(1)}, u32[]{:S(2)}, u32[]{:S(2)}) collective-permute-start(bf16[128,2688]{1,0:T(8,128)(2,1)S(1)} %get-tuple-element.70), channel_id=1, source_target_pairs={{0,2},{1,3},{4,6},{5,7},{8,10},{9,11},{12,14},{13,15},{16,18},{17,... | collective-permute-start | bytes 2064392 | tf_op jit(solution)/shard_map/ppermute | solution.py:288
  3.8 15.4 %copy-start.11 = (f32[2688]{0:T(1024)S(1)}, f32[2688]{0:T(1024)}, u32[]{:S(2)}) copy-start(f32[2688]{0:T(1024)} %param.9) | copy-start | bytes 32260
  3.8 17.0 %collective-permute-start.1 = (bf16[128,2688]{1,0:T(8,128)(2,1)S(1)}, bf16[128,2688]{1,0:T(8,128)(2,1)}, u32[]{:S(2)}, u32[]{:S(2)}) collective-permute-start(bf16[128,2688]{1,0:T(8,128)(2,1)S(1)} %get-tuple-element.69), channel_id=1, source_target_pairs={{0,130},{1,131},{4,134},{5,135},{8,138},{9,139},{12,142},{13,143},... | collective-permute-start | bytes 2064392 | tf_op jit(solution)/shard_map/ppermute | solution.py:288
  5.6 36.0 %all-to-all-start = ((bf16[64,2,2688]{2,1,0:T(2,128)(2,1)}), bf16[64,2,2688]{2,1,0:T(2,128)(2,1)S(1)}, u32[]{:S(2)}, u32[]{:S(2)}) async-start(bf16[64,2,2688]{2,1,0:T(2,128)(2,1)} %reshape_squeeze.6), calls=%async_computation | async-start | bytes 1376256 | tf_op jit(solution)/shard_map/all_to_all | solution.py:338
  19.0 48.7 %collective-permute-start.10 = (bf16[672,2688]{1,0:T(8,128)(2,1)}, bf16[672,2688]{1,0:T(8,128)(2,1)}, u32[]{:S(2)}, u32[]{:S(2)}) collective-permute-start(bf16[672,2688]{1,0:T(8,128)(2,1)} %refs_0_.1), channel_id=1, source_target_pairs={{0,1},{1,0},{4,5},{5,4},{8,9},{9,8},{12,13},{13,12},{16,17},{17,16... | collective-permute-start | bytes 10838024 | tf_op jit(solution)/shard_map/ppermute | solution.py:288
  19.2 22.4 %copy-start.1 = (f32[1,2688]{1,0:T(1,128)}, f32[1,2688]{1,0:T(1,128)S(1)}, u32[]{:S(2)}) copy-start(f32[1,2688]{1,0:T(1,128)S(1)} %reshape.15.gain_ref.refs_13_) | copy-start | bytes 32260
  19.3 22.3 %copy-start.2 = (s32[2]{0:T(128)}, s32[2]{0:T(128)S(1)}, u32[]{:S(2)}) copy-start(s32[2]{0:T(128)S(1)} %pad_add_fusion.place_ref) | copy-start | bytes 28
  19.3 22.3 %copy-start.4 = (bf16[16,8,2688]{2,1,0:T(8,128)(2,1)S(1)}, bf16[16,8,2688]{2,1,0:T(8,128)(2,1)}, u32[]{:S(2)}) copy-start(bf16[16,8,2688]{2,1,0:T(8,128)(2,1)} %inject_ref.1) | copy-start | bytes 2064388
  19.4 40.6 %copy-start.14 = (bf16[128,2688]{1,0:T(8,128)(2,1)}, bf16[128,2688]{1,0:T(8,128)(2,1)S(1)}, u32[]{:S(2)}) copy-start(bf16[128,2688]{1,0:T(8,128)(2,1)S(1)} %collective-permute-done.refs_2_) | copy-start | bytes 2064388
  23.6 35.7 %collective-permute-start.2 = (bf16[208,2688]{1,0:T(8,128)(2,1)}, bf16[208,2688]{1,0:T(8,128)(2,1)}, u32[]{:S(2)}, u32[]{:S(2)}) collective-permute-start(bf16[208,2688]{1,0:T(8,128)(2,1)} %get-tuple-element.68), channel_id=1, source_target_pairs={{0,2},{1,3},{4,6},{5,7},{8,10},{9,11},{12,14},{13,15},{16,18},{17,... | collective-permute-start | bytes 3354632 | tf_op jit(solution)/shard_map/ppermute | solution.py:288
  25.0 34.3 %collective-permute-start.3 = (bf16[208,2688]{1,0:T(8,128)(2,1)S(1)}, bf16[208,2688]{1,0:T(8,128)(2,1)}, u32[]{:S(2)}, u32[]{:S(2)}) collective-permute-start(bf16[208,2688]{1,0:T(8,128)(2,1)S(1)} %get-tuple-element.67), channel_id=1, source_target_pairs={{0,130},{1,131},{4,134},{5,135},{8,138},{9,139},{12,142},{13,143},... | collective-permute-start | bytes 3354632 | tf_op jit(solution)/shard_map/ppermute | solution.py:288
  44.7 0.9 copy-start.6
  45.6 21.8 %copy-start.5 = (f32[128,2688]{1,0:T(8,128)}, f32[128,2688]{1,0:T(8,128)S(1)}, u32[]{:S(2)}) copy-start(f32[128,2688]{1,0:T(8,128)S(1)} %get-tuple-element.48.refs_11_) | copy-start | bytes 4128772
  45.6 21.8 %copy-start.7 = (f32[128,128]{1,0:T(8,128)}, f32[128,128]{1,0:T(8,128)S(1)}, u32[]{:S(2)}) copy-start(f32[128,128]{1,0:T(8,128)S(1)} %get-tuple-element.49.refs_12_) | copy-start | bytes 196612
  45.6 8.0 %collective-permute-start.4 = (bf16[128,768]{1,0:T(8,128)(2,1)S(1)}, bf16[128,768]{1,0:T(8,128)(2,1)S(1)}, u32[]{:S(2)}, u32[]{:S(2)}) collective-permute-start(bf16[128,768]{1,0:T(8,128)(2,1)S(1)} %get-tuple-element.39), channel_id=1, source_target_pairs={{0,32},{1,33},{4,36},{5,37},{8,40},{9,41},{12,44},{13,45},{16,48},... | collective-permute-start | bytes 589832 | tf_op jit(solution)/shard_map/ppermute | solution.py:288
  45.6 10.1 %collective-permute-start.5 = (bf16[128,768]{1,0:T(8,128)(2,1)S(1)}, bf16[128,768]{1,0:T(8,128)(2,1)S(1)}, u32[]{:S(2)}, u32[]{:S(2)}) collective-permute-start(bf16[128,768]{1,0:T(8,128)(2,1)S(1)} %get-tuple-element.40), channel_id=1, source_target_pairs={{0,64},{1,65},{4,68},{5,69},{8,72},{9,73},{12,76},{13,77},{16,80},... | collective-permute-start | bytes 589832 | tf_op jit(solution)/shard_map/ppermute | solution.py:288
  53.6 5.7 %collective-permute-start.6 = (bf16[128,768]{1,0:T(8,128)(2,1)S(1)}, bf16[128,768]{1,0:T(8,128)(2,1)S(1)}, u32[]{:S(2)}, u32[]{:S(2)}) collective-permute-start(bf16[128,768]{1,0:T(8,128)(2,1)S(1)} %get-tuple-element.41), channel_id=1, source_target_pairs={{0,96},{1,97},{4,100},{5,101},{8,104},{9,105},{12,108},{13,109},{1... | collective-permute-start | bytes 589832 | tf_op jit(solution)/shard_map/ppermute | solution.py:288
  59.4 8.0 %collective-permute-start.13 = (bf16[208,2688]{1,0:T(8,128)(2,1)}, bf16[208,2688]{1,0:T(8,128)(2,1)S(1)}, u32[]{:S(2)}, u32[]{:S(2)}) collective-permute-start(bf16[208,2688]{1,0:T(8,128)(2,1)} %collective-permute-done.2.refs_6_), channel_id=1, source_target_pairs={{0,1},{1,0},{4,5},{5,4},{8,9},{9,8},{12,13},{13,12},{16,17},{17,16... | collective-permute-start | bytes 3354632 | tf_op jit(solution)/shard_map/ppermute | solution.py:288
  59.5 8.3 %collective-permute-start.14 = (bf16[208,2688]{1,0:T(8,128)(2,1)}, bf16[208,2688]{1,0:T(8,128)(2,1)S(1)}, u32[]{:S(2)}, u32[]{:S(2)}) collective-permute-start(bf16[208,2688]{1,0:T(8,128)(2,1)} %collective-permute-done.3.refs_8_), channel_id=1, source_target_pairs={{0,1},{1,0},{4,5},{5,4},{8,9},{9,8},{12,13},{13,12},{16,17},{17,16... | collective-permute-start | bytes 3354632 | tf_op jit(solution)/shard_map/ppermute | solution.py:288
  60.0 4.2 %collective-permute-start.11 = (bf16[128,2688]{1,0:T(8,128)(2,1)S(1)}, bf16[128,2688]{1,0:T(8,128)(2,1)S(1)}, u32[]{:S(2)}, u32[]{:S(2)}) collective-permute-start(bf16[128,2688]{1,0:T(8,128)(2,1)S(1)} %collective-permute-done.refs_2_), channel_id=1, source_target_pairs={{0,1},{1,0},{4,5},{5,4},{8,9},{9,8},{12,13},{13,12},{16,17},{17,16... | collective-permute-start | bytes 2064392 | tf_op jit(solution)/shard_map/ppermute | solution.py:288
  60.1 5.9 %collective-permute-start.12 = (bf16[128,2688]{1,0:T(8,128)(2,1)}, bf16[128,2688]{1,0:T(8,128)(2,1)S(1)}, u32[]{:S(2)}, u32[]{:S(2)}) collective-permute-start(bf16[128,2688]{1,0:T(8,128)(2,1)} %collective-permute-done.1.refs_4_), channel_id=1, source_target_pairs={{0,1},{1,0},{4,5},{5,4},{8,9},{9,8},{12,13},{13,12},{16,17},{17,16... | collective-permute-start | bytes 2064392 | tf_op jit(solution)/shard_map/ppermute | solution.py:288
  64.2 3.6 %copy-start.15 = (bf16[128,2688]{1,0:T(8,128)(2,1)}, bf16[128,2688]{1,0:T(8,128)(2,1)S(1)}, u32[]{:S(2)}) copy-start(bf16[128,2688]{1,0:T(8,128)(2,1)S(1)} %collective-permute-done.11.refs_3_) | copy-start | bytes 2064388
  64.2 51.6 %collective-permute-start.7 = (bf16[512,768]{1,0:T(8,128)(2,1)S(1)}, bf16[512,768]{1,0:T(8,128)(2,1)S(1)}, u32[]{:S(2)}, u32[]{:S(2)}) collective-permute-start(bf16[512,768]{1,0:T(8,128)(2,1)S(1)} %pad_maximum_fusion.refs_0_), channel_id=1, source_target_pairs={{0,1},{1,0},{4,5},{5,4},{8,9},{9,8},{12,13},{13,12},{16,17},{17,16... | collective-permute-start | bytes 2359304 | tf_op jit(solution)/shard_map/ppermute | solution.py:288
  66.0 1.8 copy-start.16
  66.0 49.8 %collective-permute-start.8 = (bf16[512,768]{1,0:T(8,128)(2,1)S(1)}, bf16[512,768]{1,0:T(8,128)(2,1)S(1)}, u32[]{:S(2)}, u32[]{:S(2)}) collective-permute-start(bf16[512,768]{1,0:T(8,128)(2,1)S(1)} %pad_maximum_fusion.refs_0_), channel_id=1, source_target_pairs={{0,2},{1,3},{4,6},{5,7},{8,10},{9,11},{12,14},{13,15},{16,18},{17,... | collective-permute-start | bytes 2359304 | tf_op jit(solution)/shard_map/ppermute | solution.py:288
  67.3 1.1 copy-start.12
  67.4 48.4 %collective-permute-start.9 = (bf16[512,768]{1,0:T(8,128)(2,1)S(1)}, bf16[512,768]{1,0:T(8,128)(2,1)S(1)}, u32[]{:S(2)}, u32[]{:S(2)}) collective-permute-start(bf16[512,768]{1,0:T(8,128)(2,1)S(1)} %pad_maximum_fusion.refs_0_), channel_id=1, source_target_pairs={{0,3},{1,2},{4,7},{5,6},{8,11},{9,10},{12,15},{13,14},{16,19},{17,... | collective-permute-start | bytes 2359304 | tf_op jit(solution)/shard_map/ppermute | solution.py:288
  67.8 1.0 copy-start.13
  115.7 53.6 %copy-start = (bf16[144,672]{1,0:T(8,128)(2,1)S(1)}, bf16[144,672]{1,0:T(8,128)(2,1)}, u32[]{:S(2)}) copy-start(bf16[144,672]{1,0:T(8,128)(2,1)} %get-tuple-element.62.refs_4_) | copy-start | bytes 580612
  115.7 53.6 %copy-start.3 = (s32[2]{0:T(128)S(1)}, s32[2]{0:T(128)}, u32[]{:S(2)}) copy-start(s32[2]{0:T(128)} %copy-done.2) | copy-start | bytes 28
  115.8 53.5 %copy-start.8 = (bf16[512,768]{1,0:T(8,128)(2,1)}, bf16[512,768]{1,0:T(8,128)(2,1)S(1)}, u32[]{:S(2)}) copy-start(bf16[512,768]{1,0:T(8,128)(2,1)S(1)} %collective-permute-done.9.refs_3_) | copy-start | bytes 2359300
  115.8 8.7 %collective-permute-start.15 = (bf16[144,672]{1,0:T(8,128)(2,1)}, bf16[144,672]{1,0:T(8,128)(2,1)S(1)}, u32[]{:S(2)}, u32[]{:S(2)}) collective-permute-start(bf16[144,672]{1,0:T(8,128)(2,1)} %get-tuple-element.58), channel_id=1, source_target_pairs={{0,1},{1,0},{4,5},{5,4},{8,9},{9,8},{12,13},{13,12},{16,17},{17,16... | collective-permute-start | bytes 580616 | tf_op jit(solution)/shard_map/ppermute | solution.py:288
  119.8 8.5 %collective-permute-start.16 = (bf16[144,672]{1,0:T(8,128)(2,1)}, bf16[144,672]{1,0:T(8,128)(2,1)S(1)}, u32[]{:S(2)}, u32[]{:S(2)}) collective-permute-start(bf16[144,672]{1,0:T(8,128)(2,1)} %get-tuple-element.59), channel_id=1, source_target_pairs={{0,2},{1,3},{4,6},{5,7},{8,10},{9,11},{12,14},{13,15},{16,18},{17,... | collective-permute-start | bytes 580616 | tf_op jit(solution)/shard_map/ppermute | solution.py:288
  119.9 11.5 %collective-permute-start.17 = (bf16[144,672]{1,0:T(8,128)(2,1)}, bf16[144,672]{1,0:T(8,128)(2,1)S(1)}, u32[]{:S(2)}, u32[]{:S(2)}) collective-permute-start(bf16[144,672]{1,0:T(8,128)(2,1)} %get-tuple-element.60), channel_id=1, source_target_pairs={{0,3},{1,2},{4,7},{5,6},{8,11},{9,10},{12,15},{13,14},{16,19},{17,... | collective-permute-start | bytes 580616 | tf_op jit(solution)/shard_map/ppermute | solution.py:288
  121.3 10.1 %collective-permute-start.18 = (bf16[144,672]{1,0:T(8,128)(2,1)}, bf16[144,672]{1,0:T(8,128)(2,1)S(1)}, u32[]{:S(2)}, u32[]{:S(2)}) collective-permute-start(bf16[144,672]{1,0:T(8,128)(2,1)} %get-tuple-element.62.refs_4_), channel_id=1, source_target_pairs={{0,32},{1,33},{4,36},{5,37},{8,40},{9,41},{12,44},{13,45},{16,48},... | collective-permute-start | bytes 580616 | tf_op jit(solution)/shard_map/ppermute | solution.py:288
  122.8 12.7 %collective-permute-start.19 = (bf16[144,672]{1,0:T(8,128)(2,1)}, bf16[144,672]{1,0:T(8,128)(2,1)S(1)}, u32[]{:S(2)}, u32[]{:S(2)}) collective-permute-start(bf16[144,672]{1,0:T(8,128)(2,1)} %get-tuple-element.62.refs_4_), channel_id=1, source_target_pairs={{0,64},{1,65},{4,68},{5,69},{8,72},{9,73},{12,76},{13,77},{16,80},... | collective-permute-start | bytes 580616 | tf_op jit(solution)/shard_map/ppermute | solution.py:288
  124.5 11.6 %collective-permute-start.20 = (bf16[144,672]{1,0:T(8,128)(2,1)}, bf16[144,672]{1,0:T(8,128)(2,1)S(1)}, u32[]{:S(2)}, u32[]{:S(2)}) collective-permute-start(bf16[144,672]{1,0:T(8,128)(2,1)} %get-tuple-element.62.refs_4_), channel_id=1, source_target_pairs={{0,96},{1,97},{4,100},{5,101},{8,104},{9,105},{12,108},{13,109},{1... | collective-permute-start | bytes 580616 | tf_op jit(solution)/shard_map/ppermute | solution.py:288
  136.1 17.8 %collective-permute-start.21 = (bf16[432,672]{1,0:T(8,128)(2,1)S(1)}, bf16[432,672]{1,0:T(8,128)(2,1)S(1)}, u32[]{:S(2)}, u32[]{:S(2)}) collective-permute-start(bf16[432,672]{1,0:T(8,128)(2,1)S(1)} %pad_maximum_fusion.1.refs_8_), channel_id=1, source_target_pairs={{0,32},{1,33},{4,36},{5,37},{8,40},{9,41},{12,44},{13,45},{16,48},... | collective-permute-start | bytes 1741832 | tf_op jit(solution)/shard_map/ppermute | solution.py:288
  137.3 32.0 %collective-permute-start.22 = (bf16[432,672]{1,0:T(8,128)(2,1)S(1)}, bf16[432,672]{1,0:T(8,128)(2,1)S(1)}, u32[]{:S(2)}, u32[]{:S(2)}) collective-permute-start(bf16[432,672]{1,0:T(8,128)(2,1)S(1)} %pad_maximum_fusion.1.refs_8_), channel_id=1, source_target_pairs={{0,64},{1,65},{4,68},{5,69},{8,72},{9,73},{12,76},{13,77},{16,80},... | collective-permute-start | bytes 1741832 | tf_op jit(solution)/shard_map/ppermute | solution.py:288
  140.2 29.1 %collective-permute-start.23 = (bf16[432,672]{1,0:T(8,128)(2,1)S(1)}, bf16[432,672]{1,0:T(8,128)(2,1)S(1)}, u32[]{:S(2)}, u32[]{:S(2)}) collective-permute-start(bf16[432,672]{1,0:T(8,128)(2,1)S(1)} %pad_maximum_fusion.1.refs_8_), channel_id=1, source_target_pairs={{0,96},{1,97},{4,100},{5,101},{8,104},{9,105},{12,108},{13,109},{1... | collective-permute-start | bytes 1741832 | tf_op jit(solution)/shard_map/ppermute | solution.py:288
  175.8 40.4 %all-to-all-start.1 = ((bf16[16,48,672]{2,1,0:T(8,128)(2,1)}), bf16[16,48,672]{2,1,0:T(8,128)(2,1)S(1)}, u32[]{:S(2)}, u32[]{:S(2)}) async-start(bf16[16,48,672]{2,1,0:T(8,128)(2,1)} %shard_map.78), calls=%async_computation.1 | async-start | bytes 2359296 | tf_op jit(solution)/shard_map/all_to_all | solution.py:357
  217.3 0.7 copy-start.10
where the time goes:
time: 218 us
  waiting for transfers between devices  100 us (46%)
  Pallas kernels  56.6 us (26%)
  starting transfers between devices  50.9 us (23%)
  local copies, waits for them, and re-layouts  8.89 us (4%)
    ppermute x24, waiting for transfers between devices, move(): lax.ppermute(value, AXES, [(flat(*place), flat(*target(*place))) for plac...  55 us
    pallas_call x1, Pallas kernels, solve(): pl.pallas_call(functools.partial(solve_kernel, offsets, 64, tolerance), o...  47 us
    all_to_all x1, waiting for transfers between devices, per_device(): got = lax.all_to_all(out, AXES, 0, 0, axis_index_groups=YZ_GROUPS)  29.2 us
    ppermute x24, starting transfers between devices, move(): lax.ppermute(value, AXES, [(flat(*place), flat(*target(*place))) for plac...  26.4 us
    all_to_all x1, waiting for transfers between devices, per_device(): lax.all_to_all(states[0].reshape(sections, own, dim), 'section', 0, 0)  15.9 us
    all_to_all x1, starting transfers between devices, per_device(): lax.all_to_all(states[0].reshape(sections, own, dim), 'section', 0, 0)  13.4 us
    all_to_all x1, starting transfers between devices, per_device(): got = lax.all_to_all(out, AXES, 0, 0, axis_index_groups=YZ_GROUPS)  11.1 us
    pallas_call x1, Pallas kernels, block_sum(): pl.pallas_call(functools.partial(block_kernel, rows, 4 * small), out_shap...  6.5 us
  transfers between devices with their start and end apart: 26, of which 15 were waited for; matrix products, arithmetic and copies ran while one was open for 2% of the time, Pallas kernels for 23%

commit v1 on v0

--- a/solution.py
+++ b/solution.py
@@ -307,23 +307,11 @@
 ]
 
 
-def fetch_weight(weight):
+def fetch_weight(weight, cut):
     half = weight.shape[0] // 2
-    cuts = (0, 128, 336)
-    source, landed = weight, []
-    for low, high in zip(cuts[:-1], cuts[1:]):
-        up, down = y_move(source[low:high], 1), y_move(source[half + low : half + high], -1)
-        source, up, down = lax.optimization_barrier((source, up, down))
-        landed += [(low, up), (half + low, down)]
-    return landed
-
-
-def share_weight(weight, landed):
-    pieces, offsets = [weight, dp_move(weight, 1)], [(0, 0, weight.shape[0]), (1, 0, weight.shape[0])]
-    for start, piece in landed:
-        pieces += [piece, dp_move(piece, 1)]
-        offsets += [(2, start, piece.shape[0]), (3, start, piece.shape[0])]
-    return pieces, tuple(offsets)
+    first = y_move(weight[:cut], 1), y_move(weight[half : half + cut], -1)
+    source, first = lax.optimization_barrier((weight, first))
+    return first, (y_move(source[cut:half], 1), y_move(source[half + cut :], -1))
 
 
 def per_device(states, inject, final_cotangent, weight, norm_gain):
@@ -333,23 +321,33 @@
     own = micro_count * row_count // sections
     place = jnp.stack([section, shard]).astype(jnp.int32)
     gain = norm_gain.reshape(1, dim)
-    landed = fetch_weight(weight)
+    cut = weight.shape[0] // 84 * 16
+    first, second = fetch_weight(weight, cut)
 
     mine = lax.all_to_all(states[0].reshape(sections, own, dim), "section", 0, 0)
     x, a, q, *a_cut = prepare(place, mine, inject, gain)
 
     a_ring = jnp.concatenate([a_cut[0]] + [x_move(a_cut[step], step) for step in range(1, X)])
-    (low, up), (high, down) = landed[-2:]
-    up, down, a_ring = lax.optimization_barrier((up, down, a_ring))
-    landed[-2:] = [(low, up), (high, down)]
-    pieces, offsets = share_weight(weight, landed)
+    shared = tuple(dp_move(piece, 1) for piece in first)
+    second, shared, a_ring = lax.optimization_barrier((second, shared, a_ring))
+    half = weight.shape[0] // 2
+    pieces, offsets = [weight, dp_move(weight, 1)], [(0, 0, 2 * half), (1, 0, 2 * half)]
+    for start, piece, other in zip((0, half), first, shared):
+        pieces += [piece, other]
+        offsets += [(2, start, cut), (3, start, cut)]
+    for start, piece in zip((cut, half + cut), second):
+        pieces += [piece, dp_move(piece, 1)]
+        offsets += [(2, start, half - cut), (3, start, half - cut)]
+    offsets = tuple(offsets)
     a_parts = [a_ring] + [dp_move(a_ring, flip) for flip in (1, 2, 3)]
 
     g_parts = solve(place, pieces, offsets, a, x, q, gain, final_cotangent, TOLERANCE)
 
     (a_parts, g_parts) = lax.optimization_barrier((a_parts, g_parts))
-    far = jnp.concatenate([dp_move(g_parts[flip], flip) for flip in (1, 2, 3)])
-    own_parts = [g_parts[0]] + [x_move(g_parts[0], step) for step in range(1, X)]
+    core_part, chip_part, chip_more = (dp_move(g_parts[flip], flip) for flip in (1, 2, 3))
+    own_part, core_part = lax.optimization_barrier((g_parts[0], core_part))
+    own_parts = [g_parts[0]] + [x_move(own_part, step) for step in range(1, X)]
+    far = jnp.concatenate([core_part, chip_part, chip_more])
     far, own_parts = lax.optimization_barrier((far, own_parts))
     far_parts = [far] + [x_move(far, step) for step in range(1, X)]
     out = block_sum(place, a_parts, own_parts, far_parts)

time: 218 us -> 216 us (level)
  waiting for transfers between devices: 100 us -> 95.2 us
  starting transfers between devices: 50.9 us -> 55.1 us
  Pallas kernels: 56.6 us -> 53.2 us
    ppermute x24, starting transfers between devices: 26.4 us -> 33.8 us  [move(): lax.ppermute(value, AXES, [(flat(*place), flat(*target(*place))) for plac...]
    ppermute x24, waiting for transfers between devices: 55 us -> 50 us  [move(): lax.ppermute(value, AXES, [(flat(*place), flat(*target(*place))) for plac...]
    pallas_call x1, Pallas kernels: 47 us -> 43.6 us  [solve(): pl.pallas_call(functools.partial(solve_kernel, offsets, 64, tolerance), o...]
    all_to_all x1, starting transfers between devices: 11.1 us -> 7.82 us  [per_device(): got = lax.all_to_all(out, AXES, 0, 0, axis_index_groups=YZ_GROUPS)]
  transfers between devices with their start and end apart: 26 -> 26, of which waited for: 15 -> 15; matrix products, arithmetic and copies ran while one was open for 2% -> 2% of each run, Pallas kernels for 23% -> 22%
where the time goes in v1:
time: 216 us; the launch traced here: 214 us
  waiting for transfers between devices  95.2 us (44%)
  starting transfers between devices  55.1 us (26%)
  Pallas kernels  53.2 us (25%)
  local copies, waits for them, and re-layouts  9.21 us (4%)
    ppermute x24, waiting for transfers between devices, move(): lax.ppermute(value, AXES, [(flat(*place), flat(*target(*place))) for plac...  50 us
    pallas_call x1, Pallas kernels, solve(): pl.pallas_call(functools.partial(solve_kernel, offsets, 64, tolerance), o...  43.6 us
    ppermute x24, starting transfers between devices, move(): lax.ppermute(value, AXES, [(flat(*place), flat(*target(*place))) for plac...  33.8 us
    all_to_all x1, waiting for transfers between devices, per_device(): got = lax.all_to_all(out, AXES, 0, 0, axis_index_groups=YZ_GROUPS)  29.2 us
    all_to_all x1, waiting for transfers between devices, per_device(): lax.all_to_all(states[0].reshape(sections, own, dim), 'section', 0, 0)  15.9 us
    all_to_all x1, starting transfers between devices, per_device(): lax.all_to_all(states[0].reshape(sections, own, dim), 'section', 0, 0)  13.4 us
    all_to_all x1, starting transfers between devices, per_device(): got = lax.all_to_all(out, AXES, 0, 0, axis_index_groups=YZ_GROUPS)  7.82 us
    pallas_call x1, Pallas kernels, block_sum(): pl.pallas_call(functools.partial(block_kernel, rows, 4 * small), out_shap...  6.5 us
  transfers between devices with their start and end apart: 26, of which 15 were waited for; matrix products, arithmetic and copies ran while one was open for 2% of the time, Pallas kernels for 22%

profile of v1, /device:TPU:8, one launch (start us, length us, event | category | flops | bytes accessed | tf_op | source)
XLA Modules:
  0.0 214.2 jit_solution(16424575025376400631)
XLA Ops:
  0.6 1.5 fusion.2
  2.1 1.7 collective-permute-start
  3.8 0.7 collective-permute-start.1
  4.5 1.1 reshape_squeeze.6
  5.6 13.4 %all-to-all-start = ((bf16[64,2,2688]{2,1,0:T(2,128)(2,1)}), bf16[64,2,2688]{2,1,0:T(2,128)(2,1)S(1)}, u32[]{:S(2)}, u32[]{:S(2)}) async-start(bf16[64,2,2688]{2,1,0:T(2,128)(2,1)} %reshape_squeeze.6), calls=%async_computation | async-start | bytes 1376256 | tf_op jit(solution)/shard_map/all_to_all | solution.py:327
  19.4 1.4 collective-permute-done.1.refs_4_
  20.8 2.8 %fusion.1 = (bf16[208,2688]{1,0:T(8,128)(2,1)S(1)}, bf16[208,2688]{1,0:T(8,128)(2,1)}) fusion(bf16[672,2688]{1,0:T(8,128)(2,1)} %refs_0_.1), kind=kLoop, calls=%fused_computation.9 | loop fusion | bytes 4472832 | tf_op jit(solution)/shard_map/slice | solution.py:314
  23.6 1.4 collective-permute-start.2
  25.0 0.6 collective-permute-start.3
  25.6 15.9 %all-to-all-done.states_ref = bf16[64,2,2688]{2,1,0:T(2,128)(2,1)S(1)} async-done(((bf16[64,2,2688]{2,1,0:T(2,128)(2,1)}), bf16[64,2,2688]{2,1,0:T(2,128)(2,1)S(1)}, u32[]{:S(2)}, u32[]{:S(2)}) %all-to-all-start) | async-done | bytes 688160 | tf_op jit(solution)/shard_map/all_to_all | solution.py:327
  41.6 3.1 %shard_map.76 = (f32[128,2688]{1,0:T(8,128)S(1)}, bf16[128,2688]{1,0:T(8,128)(2,1)S(1)}, f32[128,128]{1,0:T(8,128)S(1)}, bf16[128,768]{1,0:T(8,128)(2,1)S(1)}, b...) custom-call(s32[2]{0:T(128)S(1)} %pad_add_fusion.place_ref, ...), custom_call_target="tpu_custom_call" | custom-call | flops 20000000000 | bytes 4194304 | tf_op jit(solution)/shard_map/pallas_call | solution.py:62
  44.7 0.9 copy-done.6
  45.6 4.2 %collective-permute-start.7 = (bf16[128,768]{1,0:T(8,128)(2,1)S(1)}, bf16[128,768]{1,0:T(8,128)(2,1)S(1)}, u32[]{:S(2)}, u32[]{:S(2)}) collective-permute-start(bf16[128,768]{1,0:T(8,128)(2,1)S(1)} %get-tuple-element.42), channel_id=1, source_target_pairs={{0,64},{1,65},{4,68},{5,69},{8,72},{9,73},{12,76},{13,77},{16,80},... | collective-permute-start | bytes 589832 | tf_op jit(solution)/shard_map/ppermute | solution.py:288
  49.9 3.8 %collective-permute-done.6 = bf16[128,768]{1,0:T(8,128)(2,1)S(1)} collective-permute-done((bf16[128,768]{1,0:T(8,128)(2,1)S(1)}, bf16[128,768]{1,0:T(8,128)(2,1)S(1)}, u32[]{:S(2)}, u32[]{:S(2)}) %collective-permute-start.6) | collective-permute-done | bytes 196640 | tf_op jit(solution)/shard_map/ppermute | solution.py:288
  53.7 0.6 collective-permute-start.8
  54.2 1.5 collective-permute-done.7
  55.8 3.6 %collective-permute-done.8 = bf16[128,768]{1,0:T(8,128)(2,1)S(1)} collective-permute-done((bf16[128,768]{1,0:T(8,128)(2,1)S(1)}, bf16[128,768]{1,0:T(8,128)(2,1)S(1)}, u32[]{:S(2)}, u32[]{:S(2)}) %collective-permute-start.8) | collective-permute-done | bytes 196640 | tf_op jit(solution)/shard_map/ppermute | solution.py:288
  59.4 2.3 %collective-permute-done.5.refs_5_ = bf16[128,2688]{1,0:T(8,128)(2,1)S(1)} collective-permute-done((bf16[128,2688]{1,0:T(8,128)(2,1)}, bf16[128,2688]{1,0:T(8,128)(2,1)S(1)}, u32[]{:S(2)}, u32[]{:S(2)}) %collective-permute-start.5) | collective-permute-done | bytes 688160 | tf_op jit(solution)/shard_map/ppermute | solution.py:288
  61.7 0.2 collective-permute-start.13
  61.9 0.4 collective-permute-start.14
  62.3 0.3 copy-done.16
  62.6 1.3 collective-permute-start.10
  63.9 0.1 collective-permute-start.11
  64.1 0.7 collective-permute-done.13.refs_7_
  64.8 0.2 collective-permute-start.9
  65.0 1.4 collective-permute-done.14.refs_9_
  66.4 1.0 copy-done.13
  67.4 43.6 %shard_map.77 = (bf16[144,672]{1,0:T(8,128)(2,1)}, bf16[144,672]{1,0:T(8,128)(2,1)}, bf16[144,672]{1,0:T(8,128)(2,1)}, bf16[144,672]{1,0:T(8,128)(2,1)}) custom-call(s32[2]{0:T(128)} %copy-done.2, bf16[672,2688]{1,0:T(8,128)(2,1)} %refs_0_.1, bf16[672,2688]{1,0:T(8,128)(2,1)} %collective-permute-done.12.refs_1_, bf16[128,2688]{1,0:T(8,128)(2,1)} %copy-done.14, ...), custom_call_target="tpu_custom_call" | custom-call | flops 40000000000 | bytes 16777216 | tf_op jit(solution)/shard_map/pallas_call | solution.py:202
  111.1 3.5 %collective-permute-start.15 = (bf16[144,672]{1,0:T(8,128)(2,1)}, bf16[144,672]{1,0:T(8,128)(2,1)S(1)}, u32[]{:S(2)}, u32[]{:S(2)}) collective-permute-start(bf16[144,672]{1,0:T(8,128)(2,1)} %get-tuple-element.61), channel_id=1, source_target_pairs={{0,1},{1,0},{4,5},{5,4},{8,9},{9,8},{12,13},{13,12},{16,17},{17,16... | collective-permute-start | bytes 580616 | tf_op jit(solution)/shard_map/ppermute | solution.py:288
  114.6 1.3 collective-permute-start.16
  115.9 0.1 collective-permute-start.17
  116.1 8.1 %collective-permute-start.18 = (bf16[144,672]{1,0:T(8,128)(2,1)}, bf16[144,672]{1,0:T(8,128)(2,1)S(1)}, u32[]{:S(2)}, u32[]{:S(2)}) collective-permute-start(bf16[144,672]{1,0:T(8,128)(2,1)} %get-tuple-element.66.refs_4_), channel_id=1, source_target_pairs={{0,32},{1,33},{4,36},{5,37},{8,40},{9,41},{12,44},{13,45},{16,48},... | collective-permute-start | bytes 580616 | tf_op jit(solution)/shard_map/ppermute | solution.py:288
  124.2 2.7 %collective-permute-start.20 = (bf16[144,672]{1,0:T(8,128)(2,1)}, bf16[144,672]{1,0:T(8,128)(2,1)S(1)}, u32[]{:S(2)}, u32[]{:S(2)}) collective-permute-start(bf16[144,672]{1,0:T(8,128)(2,1)} %get-tuple-element.66.refs_4_), channel_id=1, source_target_pairs={{0,96},{1,97},{4,100},{5,101},{8,104},{9,105},{12,108},{13,109},{1... | collective-permute-start | bytes 580616 | tf_op jit(solution)/shard_map/ppermute | solution.py:288
  126.9 3.4 %collective-permute-done.18.refs_5_ = bf16[144,672]{1,0:T(8,128)(2,1)S(1)} collective-permute-done((bf16[144,672]{1,0:T(8,128)(2,1)}, bf16[144,672]{1,0:T(8,128)(2,1)S(1)}, u32[]{:S(2)}, u32[]{:S(2)}) %collective-permute-start.18) | collective-permute-done | bytes 193568 | tf_op jit(solution)/shard_map/ppermute | solution.py:288
  130.3 4.5 %collective-permute-done.19.refs_6_ = bf16[144,672]{1,0:T(8,128)(2,1)S(1)} collective-permute-done((bf16[144,672]{1,0:T(8,128)(2,1)}, bf16[144,672]{1,0:T(8,128)(2,1)S(1)}, u32[]{:S(2)}, u32[]{:S(2)}) %collective-permute-start.19) | collective-permute-done | bytes 193568 | tf_op jit(solution)/shard_map/ppermute | solution.py:288
  134.8 0.7 collective-permute-done.20.refs_7_
  135.5 2.9 %collective-permute-start.21 = (bf16[432,672]{1,0:T(8,128)(2,1)S(1)}, bf16[432,672]{1,0:T(8,128)(2,1)S(1)}, u32[]{:S(2)}, u32[]{:S(2)}) collective-permute-start(bf16[432,672]{1,0:T(8,128)(2,1)S(1)} %pad_maximum_fusion.1.refs_8_), channel_id=1, source_target_pairs={{0,32},{1,33},{4,36},{5,37},{8,40},{9,41},{12,44},{13,45},{16,48},... | collective-permute-start | bytes 1741832 | tf_op jit(solution)/shard_map/ppermute | solution.py:288
  138.4 1.2 collective-permute-start.22
  139.6 2.4 %collective-permute-start.23 = (bf16[432,672]{1,0:T(8,128)(2,1)S(1)}, bf16[432,672]{1,0:T(8,128)(2,1)S(1)}, u32[]{:S(2)}, u32[]{:S(2)}) collective-permute-start(bf16[432,672]{1,0:T(8,128)(2,1)S(1)} %pad_maximum_fusion.1.refs_8_), channel_id=1, source_target_pairs={{0,96},{1,97},{4,100},{5,101},{8,104},{9,105},{12,108},{13,109},{1... | collective-permute-start | bytes 1741832 | tf_op jit(solution)/shard_map/ppermute | solution.py:288
  141.9 11.8 %collective-permute-done.21.refs_9_ = bf16[432,672]{1,0:T(8,128)(2,1)S(1)} collective-permute-done((bf16[432,672]{1,0:T(8,128)(2,1)S(1)}, bf16[432,672]{1,0:T(8,128)(2,1)S(1)}, u32[]{:S(2)}, u32[]{:S(2)}) %collective-permute-start.21) | collective-permute-done | bytes 580640 | tf_op jit(solution)/shard_map/ppermute | solution.py:288
  153.7 14.9 %collective-permute-done.22.refs_10_ = bf16[432,672]{1,0:T(8,128)(2,1)S(1)} collective-permute-done((bf16[432,672]{1,0:T(8,128)(2,1)S(1)}, bf16[432,672]{1,0:T(8,128)(2,1)S(1)}, u32[]{:S(2)}, u32[]{:S(2)}) %collective-permute-start.22) | collective-permute-done | bytes 580640 | tf_op jit(solution)/shard_map/ppermute | solution.py:288
  168.7 6.5 %shard_map.78 = bf16[16,48,672]{2,1,0:T(8,128)(2,1)} custom-call(s32[2]{0:T(128)S(1)} %copy-done.3, bf16[512,768]{1,0:T(8,128)(2,1)S(1)} %pad_maximum_fusion.refs_0_, bf16[512,768]{1,0:T(8,128)(2,1)S(1)} %collective-permute-done.9.refs_1_, bf16[512,768]{1,0:T(8,128)(2,1)S(1)} %collective-permute-done.10.refs_2_, bf16[512,768]{1,0:T(8,128)(2,1)} %copy-done.8, ...), custom_call_target="tpu_custom_call" | custom-call | tf_op jit(solution)/shard_map/pallas_call | solution.py:260
  175.2 7.8 %all-to-all-start.1 = ((bf16[16,48,672]{2,1,0:T(8,128)(2,1)}), bf16[16,48,672]{2,1,0:T(8,128)(2,1)S(1)}, u32[]{:S(2)}, u32[]{:S(2)}) async-start(bf16[16,48,672]{2,1,0:T(8,128)(2,1)} %shard_map.78), calls=%async_computation.1 | async-start | bytes 2359296 | tf_op jit(solution)/shard_map/all_to_all | solution.py:355
  183.1 29.2 %all-to-all-done.1 = bf16[16,48,672]{2,1,0:T(8,128)(2,1)S(1)} async-done(((bf16[16,48,672]{2,1,0:T(8,128)(2,1)}), bf16[16,48,672]{2,1,0:T(8,128)(2,1)S(1)}, u32[]{:S(2)}, u32[]{:S(2)}) %all-to-all-start.1) | async-done | bytes 1032224 | tf_op jit(solution)/shard_map/all_to_all | solution.py:355
  212.5 0.1 convert_bitcast_fusion
  212.6 0.7 copy.9
  213.3 0.2 convert_reduce_fusion
  213.5 0.7 reshape.16
  (56 shorter events, 0.7 us)
Async XLA Ops:
  0.6 3.9 %copy-start.9 = (bf16[1,16,8,2688]{3,2,1,0:T(8,128)(2,1)S(1)}, bf16[1,16,8,2688]{3,2,1,0:T(8,128)(2,1)}, u32[]{:S(2)}) copy-start(bf16[1,16,8,2688]{3,2,1,0:T(8,128)(2,1)} %param.5) | copy-start | bytes 2064388
  2.1 17.3 %collective-permute-start = (bf16[128,2688]{1,0:T(8,128)(2,1)S(1)}, bf16[128,2688]{1,0:T(8,128)(2,1)S(1)}, u32[]{:S(2)}, u32[]{:S(2)}) collective-permute-start(bf16[128,2688]{1,0:T(8,128)(2,1)S(1)} %get-tuple-element.74), channel_id=1, source_target_pairs={{0,2},{1,3},{4,6},{5,7},{8,10},{9,11},{12,14},{13,15},{16,18},{17,... | collective-permute-start | bytes 2064392 | tf_op jit(solution)/shard_map/ppermute | solution.py:288
  3.8 15.4 %copy-start.11 = (f32[2688]{0:T(1024)S(1)}, f32[2688]{0:T(1024)}, u32[]{:S(2)}) copy-start(f32[2688]{0:T(1024)} %param.9) | copy-start | bytes 32260
  3.8 17.0 %collective-permute-start.1 = (bf16[128,2688]{1,0:T(8,128)(2,1)S(1)}, bf16[128,2688]{1,0:T(8,128)(2,1)}, u32[]{:S(2)}, u32[]{:S(2)}) collective-permute-start(bf16[128,2688]{1,0:T(8,128)(2,1)S(1)} %get-tuple-element.73), channel_id=1, source_target_pairs={{0,130},{1,131},{4,134},{5,135},{8,138},{9,139},{12,142},{13,143},... | collective-permute-start | bytes 2064392 | tf_op jit(solution)/shard_map/ppermute | solution.py:288
  5.6 36.0 %all-to-all-start = ((bf16[64,2,2688]{2,1,0:T(2,128)(2,1)}), bf16[64,2,2688]{2,1,0:T(2,128)(2,1)S(1)}, u32[]{:S(2)}, u32[]{:S(2)}) async-start(bf16[64,2,2688]{2,1,0:T(2,128)(2,1)} %reshape_squeeze.6), calls=%async_computation | async-start | bytes 1376256 | tf_op jit(solution)/shard_map/all_to_all | solution.py:327
  19.0 47.3 %collective-permute-start.12 = (bf16[672,2688]{1,0:T(8,128)(2,1)}, bf16[672,2688]{1,0:T(8,128)(2,1)}, u32[]{:S(2)}, u32[]{:S(2)}) collective-permute-start(bf16[672,2688]{1,0:T(8,128)(2,1)} %refs_0_.1), channel_id=1, source_target_pairs={{0,1},{1,0},{4,5},{5,4},{8,9},{9,8},{12,13},{13,12},{16,17},{17,16... | collective-permute-start | bytes 10838024 | tf_op jit(solution)/shard_map/ppermute | solution.py:288
  19.2 22.4 %copy-start.1 = (f32[1,2688]{1,0:T(1,128)}, f32[1,2688]{1,0:T(1,128)S(1)}, u32[]{:S(2)}) copy-start(f32[1,2688]{1,0:T(1,128)S(1)} %reshape.15.gain_ref.refs_13_) | copy-start | bytes 32260
  19.3 22.3 %copy-start.2 = (s32[2]{0:T(128)}, s32[2]{0:T(128)S(1)}, u32[]{:S(2)}) copy-start(s32[2]{0:T(128)S(1)} %pad_add_fusion.place_ref) | copy-start | bytes 28
  19.3 22.3 %copy-start.4 = (bf16[16,8,2688]{2,1,0:T(8,128)(2,1)S(1)}, bf16[16,8,2688]{2,1,0:T(8,128)(2,1)}, u32[]{:S(2)}) copy-start(bf16[16,8,2688]{2,1,0:T(8,128)(2,1)} %inject_ref.1) | copy-start | bytes 2064388
  19.4 36.4 %copy-start.14 = (bf16[128,2688]{1,0:T(8,128)(2,1)}, bf16[128,2688]{1,0:T(8,128)(2,1)S(1)}, u32[]{:S(2)}) copy-start(bf16[128,2688]{1,0:T(8,128)(2,1)S(1)} %collective-permute-done.refs_2_) | copy-start | bytes 2064388
  23.6 38.1 %collective-permute-start.2 = (bf16[208,2688]{1,0:T(8,128)(2,1)}, bf16[208,2688]{1,0:T(8,128)(2,1)}, u32[]{:S(2)}, u32[]{:S(2)}) collective-permute-start(bf16[208,2688]{1,0:T(8,128)(2,1)} %get-tuple-element.72), channel_id=1, source_target_pairs={{0,2},{1,3},{4,6},{5,7},{8,10},{9,11},{12,14},{13,15},{16,18},{17,... | collective-permute-start | bytes 3354632 | tf_op jit(solution)/shard_map/ppermute | solution.py:288
  25.0 36.7 %collective-permute-start.3 = (bf16[208,2688]{1,0:T(8,128)(2,1)S(1)}, bf16[208,2688]{1,0:T(8,128)(2,1)}, u32[]{:S(2)}, u32[]{:S(2)}) collective-permute-start(bf16[208,2688]{1,0:T(8,128)(2,1)S(1)} %get-tuple-element.71), channel_id=1, source_target_pairs={{0,130},{1,131},{4,134},{5,135},{8,138},{9,139},{12,142},{13,143},... | collective-permute-start | bytes 3354632 | tf_op jit(solution)/shard_map/ppermute | solution.py:288
  44.7 0.9 copy-start.6
  45.6 18.4 %copy-start.5 = (f32[128,2688]{1,0:T(8,128)}, f32[128,2688]{1,0:T(8,128)S(1)}, u32[]{:S(2)}) copy-start(f32[128,2688]{1,0:T(8,128)S(1)} %get-tuple-element.50.refs_11_) | copy-start | bytes 4128772
  45.6 19.1 %copy-start.7 = (f32[128,128]{1,0:T(8,128)}, f32[128,128]{1,0:T(8,128)S(1)}, u32[]{:S(2)}) copy-start(f32[128,128]{1,0:T(8,128)S(1)} %get-tuple-element.51.refs_12_) | copy-start | bytes 196612
  45.6 8.0 %collective-permute-start.6 = (bf16[128,768]{1,0:T(8,128)(2,1)S(1)}, bf16[128,768]{1,0:T(8,128)(2,1)S(1)}, u32[]{:S(2)}, u32[]{:S(2)}) collective-permute-start(bf16[128,768]{1,0:T(8,128)(2,1)S(1)} %get-tuple-element.41), channel_id=1, source_target_pairs={{0,32},{1,33},{4,36},{5,37},{8,40},{9,41},{12,44},{13,45},{16,48},... | collective-permute-start | bytes 589832 | tf_op jit(solution)/shard_map/ppermute | solution.py:288
  45.6 10.1 %collective-permute-start.7 = (bf16[128,768]{1,0:T(8,128)(2,1)S(1)}, bf16[128,768]{1,0:T(8,128)(2,1)S(1)}, u32[]{:S(2)}, u32[]{:S(2)}) collective-permute-start(bf16[128,768]{1,0:T(8,128)(2,1)S(1)} %get-tuple-element.42), channel_id=1, source_target_pairs={{0,64},{1,65},{4,68},{5,69},{8,72},{9,73},{12,76},{13,77},{16,80},... | collective-permute-start | bytes 589832 | tf_op jit(solution)/shard_map/ppermute | solution.py:288
  53.7 5.7 %collective-permute-start.8 = (bf16[128,768]{1,0:T(8,128)(2,1)S(1)}, bf16[128,768]{1,0:T(8,128)(2,1)S(1)}, u32[]{:S(2)}, u32[]{:S(2)}) collective-permute-start(bf16[128,768]{1,0:T(8,128)(2,1)S(1)} %get-tuple-element.43), channel_id=1, source_target_pairs={{0,96},{1,97},{4,100},{5,101},{8,104},{9,105},{12,108},{13,109},{1... | collective-permute-start | bytes 589832 | tf_op jit(solution)/shard_map/ppermute | solution.py:288
  55.8 3.6 %collective-permute-start.4 = (bf16[128,2688]{1,0:T(8,128)(2,1)S(1)}, bf16[128,2688]{1,0:T(8,128)(2,1)S(1)}, u32[]{:S(2)}, u32[]{:S(2)}) collective-permute-start(bf16[128,2688]{1,0:T(8,128)(2,1)S(1)} %collective-permute-done.refs_2_), channel_id=1, source_target_pairs={{0,1},{1,0},{4,5},{5,4},{8,9},{9,8},{12,13},{13,12},{16,17},{17,16... | collective-permute-start | bytes 2064392 | tf_op jit(solution)/shard_map/ppermute | solution.py:288
  59.3 2.4 %collective-permute-start.5 = (bf16[128,2688]{1,0:T(8,128)(2,1)}, bf16[128,2688]{1,0:T(8,128)(2,1)S(1)}, u32[]{:S(2)}, u32[]{:S(2)}) collective-permute-start(bf16[128,2688]{1,0:T(8,128)(2,1)} %collective-permute-done.1.refs_4_), channel_id=1, source_target_pairs={{0,1},{1,0},{4,5},{5,4},{8,9},{9,8},{12,13},{13,12},{16,17},{17,16... | collective-permute-start | bytes 2064392 | tf_op jit(solution)/shard_map/ppermute | solution.py:288
  59.4 7.0 %copy-start.15 = (bf16[128,2688]{1,0:T(8,128)(2,1)}, bf16[128,2688]{1,0:T(8,128)(2,1)S(1)}, u32[]{:S(2)}) copy-start(bf16[128,2688]{1,0:T(8,128)(2,1)S(1)} %collective-permute-done.4.refs_3_) | copy-start | bytes 2064388
  61.7 0.9 copy-start.16
  61.7 3.1 %collective-permute-start.13 = (bf16[208,2688]{1,0:T(8,128)(2,1)}, bf16[208,2688]{1,0:T(8,128)(2,1)S(1)}, u32[]{:S(2)}, u32[]{:S(2)}) collective-permute-start(bf16[208,2688]{1,0:T(8,128)(2,1)} %collective-permute-done.2.refs_6_), channel_id=1, source_target_pairs={{0,1},{1,0},{4,5},{5,4},{8,9},{9,8},{12,13},{13,12},{16,17},{17,16... | collective-permute-start | bytes 3354632 | tf_op jit(solution)/shard_map/ppermute | solution.py:288
  61.9 4.4 %collective-permute-start.14 = (bf16[208,2688]{1,0:T(8,128)(2,1)}, bf16[208,2688]{1,0:T(8,128)(2,1)S(1)}, u32[]{:S(2)}, u32[]{:S(2)}) collective-permute-start(bf16[208,2688]{1,0:T(8,128)(2,1)} %collective-permute-done.3.refs_8_), channel_id=1, source_target_pairs={{0,1},{1,0},{4,5},{5,4},{8,9},{9,8},{12,13},{13,12},{16,17},{17,16... | collective-permute-start | bytes 3354632 | tf_op jit(solution)/shard_map/ppermute | solution.py:288
  62.6 48.5 %collective-permute-start.10 = (bf16[512,768]{1,0:T(8,128)(2,1)S(1)}, bf16[512,768]{1,0:T(8,128)(2,1)S(1)}, u32[]{:S(2)}, u32[]{:S(2)}) collective-permute-start(bf16[512,768]{1,0:T(8,128)(2,1)S(1)} %pad_maximum_fusion.refs_0_), channel_id=1, source_target_pairs={{0,2},{1,3},{4,6},{5,7},{8,10},{9,11},{12,14},{13,15},{16,18},{17,... | collective-permute-start | bytes 2359304 | tf_op jit(solution)/shard_map/ppermute | solution.py:288
  63.9 47.1 %collective-permute-start.11 = (bf16[512,768]{1,0:T(8,128)(2,1)S(1)}, bf16[512,768]{1,0:T(8,128)(2,1)S(1)}, u32[]{:S(2)}, u32[]{:S(2)}) collective-permute-start(bf16[512,768]{1,0:T(8,128)(2,1)S(1)} %pad_maximum_fusion.refs_0_), channel_id=1, source_target_pairs={{0,3},{1,2},{4,7},{5,6},{8,11},{9,10},{12,15},{13,14},{16,19},{17,... | collective-permute-start | bytes 2359304 | tf_op jit(solution)/shard_map/ppermute | solution.py:288
  64.8 1.6 copy-start.12
  64.8 46.3 %collective-permute-start.9 = (bf16[512,768]{1,0:T(8,128)(2,1)S(1)}, bf16[512,768]{1,0:T(8,128)(2,1)S(1)}, u32[]{:S(2)}, u32[]{:S(2)}) collective-permute-start(bf16[512,768]{1,0:T(8,128)(2,1)S(1)} %pad_maximum_fusion.refs_0_), channel_id=1, source_target_pairs={{0,1},{1,0},{4,5},{5,4},{8,9},{9,8},{12,13},{13,12},{16,17},{17,16... | collective-permute-start | bytes 2359304 | tf_op jit(solution)/shard_map/ppermute | solution.py:288
  66.4 1.0 copy-start.13
  111.0 57.7 %copy-start = (bf16[144,672]{1,0:T(8,128)(2,1)S(1)}, bf16[144,672]{1,0:T(8,128)(2,1)}, u32[]{:S(2)}) copy-start(bf16[144,672]{1,0:T(8,128)(2,1)} %get-tuple-element.66.refs_4_) | copy-start | bytes 580612
  111.0 57.6 %copy-start.3 = (s32[2]{0:T(128)S(1)}, s32[2]{0:T(128)}, u32[]{:S(2)}) copy-start(s32[2]{0:T(128)} %copy-done.2) | copy-start | bytes 28
  111.1 57.6 %copy-start.8 = (bf16[512,768]{1,0:T(8,128)(2,1)}, bf16[512,768]{1,0:T(8,128)(2,1)S(1)}, u32[]{:S(2)}) copy-start(bf16[512,768]{1,0:T(8,128)(2,1)S(1)} %collective-permute-done.11.refs_3_) | copy-start | bytes 2359300
  111.1 5.0 %collective-permute-start.15 = (bf16[144,672]{1,0:T(8,128)(2,1)}, bf16[144,672]{1,0:T(8,128)(2,1)S(1)}, u32[]{:S(2)}, u32[]{:S(2)}) collective-permute-start(bf16[144,672]{1,0:T(8,128)(2,1)} %get-tuple-element.61), channel_id=1, source_target_pairs={{0,1},{1,0},{4,5},{5,4},{8,9},{9,8},{12,13},{13,12},{16,17},{17,16... | collective-permute-start | bytes 580616 | tf_op jit(solution)/shard_map/ppermute | solution.py:288
  114.6 12.3 %collective-permute-start.16 = (bf16[144,672]{1,0:T(8,128)(2,1)}, bf16[144,672]{1,0:T(8,128)(2,1)S(1)}, u32[]{:S(2)}, u32[]{:S(2)}) collective-permute-start(bf16[144,672]{1,0:T(8,128)(2,1)} %get-tuple-element.63), channel_id=1, source_target_pairs={{0,2},{1,3},{4,6},{5,7},{8,10},{9,11},{12,14},{13,15},{16,18},{17,... | collective-permute-start | bytes 580616 | tf_op jit(solution)/shard_map/ppermute | solution.py:288
  115.9 10.9 %collective-permute-start.17 = (bf16[144,672]{1,0:T(8,128)(2,1)}, bf16[144,672]{1,0:T(8,128)(2,1)S(1)}, u32[]{:S(2)}, u32[]{:S(2)}) collective-permute-start(bf16[144,672]{1,0:T(8,128)(2,1)} %get-tuple-element.64), channel_id=1, source_target_pairs={{0,3},{1,2},{4,7},{5,6},{8,11},{9,10},{12,15},{13,14},{16,19},{17,... | collective-permute-start | bytes 580616 | tf_op jit(solution)/shard_map/ppermute | solution.py:288
  116.1 14.3 %collective-permute-start.18 = (bf16[144,672]{1,0:T(8,128)(2,1)}, bf16[144,672]{1,0:T(8,128)(2,1)S(1)}, u32[]{:S(2)}, u32[]{:S(2)}) collective-permute-start(bf16[144,672]{1,0:T(8,128)(2,1)} %get-tuple-element.66.refs_4_), channel_id=1, source_target_pairs={{0,32},{1,33},{4,36},{5,37},{8,40},{9,41},{12,44},{13,45},{16,48},... | collective-permute-start | bytes 580616 | tf_op jit(solution)/shard_map/ppermute | solution.py:288
  124.2 10.6 %collective-permute-start.19 = (bf16[144,672]{1,0:T(8,128)(2,1)}, bf16[144,672]{1,0:T(8,128)(2,1)S(1)}, u32[]{:S(2)}, u32[]{:S(2)}) collective-permute-start(bf16[144,672]{1,0:T(8,128)(2,1)} %get-tuple-element.66.refs_4_), channel_id=1, source_target_pairs={{0,64},{1,65},{4,68},{5,69},{8,72},{9,73},{12,76},{13,77},{16,80},... | collective-permute-start | bytes 580616 | tf_op jit(solution)/shard_map/ppermute | solution.py:288
  124.2 11.3 %collective-permute-start.20 = (bf16[144,672]{1,0:T(8,128)(2,1)}, bf16[144,672]{1,0:T(8,128)(2,1)S(1)}, u32[]{:S(2)}, u32[]{:S(2)}) collective-permute-start(bf16[144,672]{1,0:T(8,128)(2,1)} %get-tuple-element.66.refs_4_), channel_id=1, source_target_pairs={{0,96},{1,97},{4,100},{5,101},{8,104},{9,105},{12,108},{13,109},{1... | collective-permute-start | bytes 580616 | tf_op jit(solution)/shard_map/ppermute | solution.py:288
  135.5 18.2 %collective-permute-start.21 = (bf16[432,672]{1,0:T(8,128)(2,1)S(1)}, bf16[432,672]{1,0:T(8,128)(2,1)S(1)}, u32[]{:S(2)}, u32[]{:S(2)}) collective-permute-start(bf16[432,672]{1,0:T(8,128)(2,1)S(1)} %pad_maximum_fusion.1.refs_8_), channel_id=1, source_target_pairs={{0,32},{1,33},{4,36},{5,37},{8,40},{9,41},{12,44},{13,45},{16,48},... | collective-permute-start | bytes 1741832 | tf_op jit(solution)/shard_map/ppermute | solution.py:288
  138.4 30.3 %collective-permute-start.22 = (bf16[432,672]{1,0:T(8,128)(2,1)S(1)}, bf16[432,672]{1,0:T(8,128)(2,1)S(1)}, u32[]{:S(2)}, u32[]{:S(2)}) collective-permute-start(bf16[432,672]{1,0:T(8,128)(2,1)S(1)} %pad_maximum_fusion.1.refs_8_), channel_id=1, source_target_pairs={{0,64},{1,65},{4,68},{5,69},{8,72},{9,73},{12,76},{13,77},{16,80},... | collective-permute-start | bytes 1741832 | tf_op jit(solution)/shard_map/ppermute | solution.py:288
  139.6 29.1 %collective-permute-start.23 = (bf16[432,672]{1,0:T(8,128)(2,1)S(1)}, bf16[432,672]{1,0:T(8,128)(2,1)S(1)}, u32[]{:S(2)}, u32[]{:S(2)}) collective-permute-start(bf16[432,672]{1,0:T(8,128)(2,1)S(1)} %pad_maximum_fusion.1.refs_8_), channel_id=1, source_target_pairs={{0,96},{1,97},{4,100},{5,101},{8,104},{9,105},{12,108},{13,109},{1... | collective-permute-start | bytes 1741832 | tf_op jit(solution)/shard_map/ppermute | solution.py:288
  175.2 37.1 %all-to-all-start.1 = ((bf16[16,48,672]{2,1,0:T(8,128)(2,1)}), bf16[16,48,672]{2,1,0:T(8,128)(2,1)S(1)}, u32[]{:S(2)}, u32[]{:S(2)}) async-start(bf16[16,48,672]{2,1,0:T(8,128)(2,1)} %shard_map.78), calls=%async_computation.1 | async-start | bytes 2359296 | tf_op jit(solution)/shard_map/all_to_all | solution.py:355
  213.4 0.7 copy-start.10

commit v2 on v1

--- a/solution.py
+++ b/solution.py
@@ -11,6 +11,7 @@
 EPSILON = 1e-06
 TOLERANCE = 2.0**-10
 LANES = 128
+HALVES = (64, 224)
 WIDE = 512
 AXES = ("section", "dp")
 Y_HI, X, Z, Y_LO, CORE = 2, 4, 8, 2, 2
@@ -215,14 +216,25 @@
 
 
 def block_kernel(rows, dim, place_ref, *refs):
-    a_refs, own_refs, far_refs = refs[:4], refs[4:8], refs[8:12]
+    a_refs, own_refs, far_refs, half_refs = refs[:4], refs[4:7], refs[7:10], refs[10:12]
     out_ref, a, g, sems = refs[12:]
     small, part = dim // 4, dim // 64
     tall = rows + 16
     copies = [pltpu.make_async_copy(a_refs[flip], a.at[flip], sems.at[flip]) for flip in range(4)]
-    for step in range(X):
-        copies.append(pltpu.make_async_copy(own_refs[step], g.at[pl.ds(step * tall, tall)], sems.at[4 + step]))
-        copies.append(pltpu.make_async_copy(far_refs[step], g.at[pl.ds((4 + 3 * step) * tall, 3 * tall)], sems.at[8 + step]))
+    for n, step in enumerate((0, 1, 3)):
+        copies.append(pltpu.make_async_copy(own_refs[n], g.at[pl.ds(step * tall, tall)], sems.at[4 + n]))
+        copies.append(pltpu.make_async_copy(far_refs[n], g.at[pl.ds((4 + 3 * step) * tall, 3 * tall)], sems.at[7 + n]))
+    own_cut, far_cut = HALVES
+    first, last = half_refs
+    for n, (ref, start, length, at) in enumerate(
+        (
+            (first, 0, own_cut, 2 * tall),
+            (first, own_cut, far_cut, 10 * tall),
+            (last, 0, tall - own_cut, 2 * tall + own_cut),
+            (last, tall - own_cut, 3 * tall - far_cut, 10 * tall + far_cut),
+        )
+    ):
+        copies.append(pltpu.make_async_copy(ref.at[pl.ds(start, length)], g.at[pl.ds(at, length)], sems.at[10 + n]))
     for copy in copies:
         copy.start()
     for copy in copies:
@@ -254,7 +266,7 @@
         out_ref[k] = jnp.concatenate([block[k * part : (k + 1) * part], line, gain[0:5]], axis=0).astype(bf16)
 
 
-def block_sum(place, a_parts, own_parts, far_parts):
+def block_sum(place, a_parts, own_parts, far_parts, halves):
     rows, small = a_parts[0].shape[0] // X, own_parts[0].shape[1]
     hold = pl.BlockSpec(memory_space=pl.ANY)
     return pl.pallas_call(
@@ -265,10 +277,10 @@
         scratch_shapes=[
             pltpu.VMEM((4,) + a_parts[0].shape, bf16),
             pltpu.VMEM((16 * (rows + 16), small), bf16),
-            pltpu.SemaphoreType.DMA((12,)),
+            pltpu.SemaphoreType.DMA((14,)),
         ],
         compiler_params=pltpu.CompilerParams(vmem_limit_bytes=48 * 2**20),
-    )(place, *a_parts, *own_parts, *far_parts)
+    )(place, *a_parts, *own_parts, *far_parts, *halves)
 
 
 def flat(y, x, z, core):
@@ -346,11 +358,16 @@
     (a_parts, g_parts) = lax.optimization_barrier((a_parts, g_parts))
     core_part, chip_part, chip_more = (dp_move(g_parts[flip], flip) for flip in (1, 2, 3))
     own_part, core_part = lax.optimization_barrier((g_parts[0], core_part))
-    own_parts = [g_parts[0]] + [x_move(own_part, step) for step in range(1, X)]
+    own_parts = [g_parts[0], x_move(own_part, 1), x_move(own_part, -1)]
     far = jnp.concatenate([core_part, chip_part, chip_more])
     far, own_parts = lax.optimization_barrier((far, own_parts))
-    far_parts = [far] + [x_move(far, step) for step in range(1, X)]
-    out = block_sum(place, a_parts, own_parts, far_parts)
+    far_parts = [far, x_move(far, 1), x_move(far, -1)]
+    own_cut, far_cut = HALVES
+    halves = [
+        x_move(jnp.concatenate([own_parts[1][:own_cut], far_parts[1][:far_cut]]), 1),
+        x_move(jnp.concatenate([own_parts[2][own_cut:], far_parts[2][far_cut:]]), -1),
+    ]
+    out = block_sum(place, a_parts, own_parts, far_parts, halves)
 
     got = lax.all_to_all(out, AXES, 0, 0, axis_index_groups=YZ_GROUPS)
     part = dim // 64

time: 216 us -> 212 us (0.981); the launches traced: 214 us -> 207 us
  starting transfers between devices: 55.1 us -> 43.7 us
  Pallas kernels: 53.2 us -> 56.6 us
    ppermute x24, starting transfers between devices: 33.8 us -> 22.7 us  [move(): lax.ppermute(value, AXES, [(flat(*place), flat(*target(*place))) for plac...]
    pallas_call x1, Pallas kernels: 43.6 us -> 46.9 us  [solve(): pl.pallas_call(functools.partial(solve_kernel, offsets, 64, tolerance), o...]
  transfers between devices with their start and end apart: 26 -> 26, of which waited for: 15 -> 17; matrix products, arithmetic and copies ran while one was open for 2% -> 2% of each run, Pallas kernels for 22% -> 24%
where the time goes in v2:
time: 212 us; the launch traced here: 207 us
  waiting for transfers between devices  96.3 us (45%)
  Pallas kernels  56.6 us (27%)
  starting transfers between devices  43.7 us (21%)
  local copies, waits for them, and re-layouts  9.28 us (4%)
    ppermute x24, waiting for transfers between devices, move(): lax.ppermute(value, AXES, [(flat(*place), flat(*target(*place))) for plac...  50.7 us
    pallas_call x1, Pallas kernels, solve(): pl.pallas_call(functools.partial(solve_kernel, offsets, 64, tolerance), o...  46.9 us
    all_to_all x1, waiting for transfers between devices, per_device(): got = lax.all_to_all(out, AXES, 0, 0, axis_index_groups=YZ_GROUPS)  29.6 us
    ppermute x24, starting transfers between devices, move(): lax.ppermute(value, AXES, [(flat(*place), flat(*target(*place))) for plac...  22.7 us
    all_to_all x1, waiting for transfers between devices, per_device(): lax.all_to_all(states[0].reshape(sections, own, dim), 'section', 0, 0)  15.9 us
    all_to_all x1, starting transfers between devices, per_device(): lax.all_to_all(states[0].reshape(sections, own, dim), 'section', 0, 0)  13.4 us
    all_to_all x1, starting transfers between devices, per_device(): got = lax.all_to_all(out, AXES, 0, 0, axis_index_groups=YZ_GROUPS)  7.59 us
    pallas_call x1, Pallas kernels, block_sum(): pl.pallas_call(functools.partial(block_kernel, rows, 4 * small), out_shap...  6.51 us
  transfers between devices with their start and end apart: 26, of which 17 were waited for; matrix products, arithmetic and copies ran while one was open for 2% of the time, Pallas kernels for 24%

profile of v2, /device:TPU:8, one launch (start us, length us, event | category | flops | bytes accessed | tf_op | source)
XLA Modules:
  0.0 207.4 jit_solution(1688619067358192088)
XLA Ops:
  0.6 1.5 fusion.2
  2.1 1.7 collective-permute-start
  3.8 0.7 collective-permute-start.1
  4.5 1.1 reshape_squeeze.6
  5.6 13.4 %all-to-all-start = ((bf16[64,2,2688]{2,1,0:T(2,128)(2,1)}), bf16[64,2,2688]{2,1,0:T(2,128)(2,1)S(1)}, u32[]{:S(2)}, u32[]{:S(2)}) async-start(bf16[64,2,2688]{2,1,0:T(2,128)(2,1)} %reshape_squeeze.6), calls=%async_computation | async-start | bytes 1376256 | tf_op jit(solution)/shard_map/all_to_all | solution.py:339
  19.4 1.4 collective-permute-done.1.refs_4_
  20.8 2.8 %fusion.1 = (bf16[208,2688]{1,0:T(8,128)(2,1)S(1)}, bf16[208,2688]{1,0:T(8,128)(2,1)}) fusion(bf16[672,2688]{1,0:T(8,128)(2,1)} %refs_0_.1), kind=kLoop, calls=%fused_computation.11 | loop fusion | bytes 4472832 | tf_op jit(solution)/shard_map/slice | solution.py:326
  23.6 1.4 collective-permute-start.2
  25.0 0.6 collective-permute-start.3
  25.6 15.9 %all-to-all-done.states_ref = bf16[64,2,2688]{2,1,0:T(2,128)(2,1)S(1)} async-done(((bf16[64,2,2688]{2,1,0:T(2,128)(2,1)}), bf16[64,2,2688]{2,1,0:T(2,128)(2,1)S(1)}, u32[]{:S(2)}, u32[]{:S(2)}) %all-to-all-start) | async-done | bytes 688160 | tf_op jit(solution)/shard_map/all_to_all | solution.py:339
  41.6 3.1 %shard_map.76 = (f32[128,2688]{1,0:T(8,128)S(1)}, bf16[128,2688]{1,0:T(8,128)(2,1)S(1)}, f32[128,128]{1,0:T(8,128)S(1)}, bf16[128,768]{1,0:T(8,128)(2,1)S(1)}, b...) custom-call(s32[2]{0:T(128)S(1)} %pad_add_fusion.place_ref, ...), custom_call_target="tpu_custom_call" | custom-call | flops 20000000000 | bytes 4194304 | tf_op jit(solution)/shard_map/pallas_call | solution.py:63
  44.7 0.9 copy-done.6
  45.6 4.2 %collective-permute-start.7 = (bf16[128,768]{1,0:T(8,128)(2,1)S(1)}, bf16[128,768]{1,0:T(8,128)(2,1)S(1)}, u32[]{:S(2)}, u32[]{:S(2)}) collective-permute-start(bf16[128,768]{1,0:T(8,128)(2,1)S(1)} %get-tuple-element.41), channel_id=1, source_target_pairs={{0,64},{1,65},{4,68},{5,69},{8,72},{9,73},{12,76},{13,77},{16,80},... | collective-permute-start | bytes 589832 | tf_op jit(solution)/shard_map/ppermute | solution.py:300
  49.9 3.8 %collective-permute-done.6 = bf16[128,768]{1,0:T(8,128)(2,1)S(1)} collective-permute-done((bf16[128,768]{1,0:T(8,128)(2,1)S(1)}, bf16[128,768]{1,0:T(8,128)(2,1)S(1)}, u32[]{:S(2)}, u32[]{:S(2)}) %collective-permute-start.6) | collective-permute-done | bytes 196640 | tf_op jit(solution)/shard_map/ppermute | solution.py:300
  53.7 0.6 collective-permute-start.8
  54.2 1.5 collective-permute-done.7
  55.8 3.6 %collective-permute-done.8 = bf16[128,768]{1,0:T(8,128)(2,1)S(1)} collective-permute-done((bf16[128,768]{1,0:T(8,128)(2,1)S(1)}, bf16[128,768]{1,0:T(8,128)(2,1)S(1)}, u32[]{:S(2)}, u32[]{:S(2)}) %collective-permute-start.8) | collective-permute-done | bytes 196640 | tf_op jit(solution)/shard_map/ppermute | solution.py:300
  59.4 2.3 %collective-permute-done.5.refs_5_ = bf16[128,2688]{1,0:T(8,128)(2,1)S(1)} collective-permute-done((bf16[128,2688]{1,0:T(8,128)(2,1)}, bf16[128,2688]{1,0:T(8,128)(2,1)S(1)}, u32[]{:S(2)}, u32[]{:S(2)}) %collective-permute-start.5) | collective-permute-done | bytes 688160 | tf_op jit(solution)/shard_map/ppermute | solution.py:300
  61.7 0.2 collective-permute-start.13
  61.9 0.4 collective-permute-start.14
  62.3 0.3 copy-done.16
  62.6 1.3 collective-permute-start.10
  63.9 0.1 collective-permute-start.11
  64.1 0.7 collective-permute-done.13.refs_7_
  64.8 0.2 collective-permute-start.9
  65.0 1.4 collective-permute-done.14.refs_9_
  66.4 1.0 copy-done.13
  67.4 46.9 %shard_map.77 = (bf16[144,672]{1,0:T(8,128)(2,1)}, bf16[144,672]{1,0:T(8,128)(2,1)}, bf16[144,672]{1,0:T(8,128)(2,1)}, bf16[144,672]{1,0:T(8,128)(2,1)}) custom-call(s32[2]{0:T(128)} %copy-done.2, bf16[672,2688]{1,0:T(8,128)(2,1)} %refs_0_.1, bf16[672,2688]{1,0:T(8,128)(2,1)} %collective-permute-done.12.refs_1_, bf16[128,2688]{1,0:T(8,128)(2,1)} %copy-done.14, ...), custom_call_target="tpu_custom_call" | custom-call | flops 40000000000 | bytes 16777216 | tf_op jit(solution)/shard_map/pallas_call | solution.py:203
  114.5 1.5 collective-permute-start.16
  116.0 0.4 collective-permute-start.17
  116.3 1.5 collective-permute-start.18
  117.8 1.7 collective-permute-start.19
  119.6 3.4 %collective-permute-done.16 = bf16[144,672]{1,0:T(8,128)(2,1)S(1)} collective-permute-done((bf16[144,672]{1,0:T(8,128)(2,1)}, bf16[144,672]{1,0:T(8,128)(2,1)S(1)}, u32[]{:S(2)}, u32[]{:S(2)}) %collective-permute-start.16) | collective-permute-done | bytes 193568 | tf_op jit(solution)/shard_map/ppermute | solution.py:300
  123.0 3.8 %collective-permute-done.17 = bf16[144,672]{1,0:T(8,128)(2,1)S(1)} collective-permute-done((bf16[144,672]{1,0:T(8,128)(2,1)}, bf16[144,672]{1,0:T(8,128)(2,1)S(1)}, u32[]{:S(2)}, u32[]{:S(2)}) %collective-permute-start.17) | collective-permute-done | bytes 193568 | tf_op jit(solution)/shard_map/ppermute | solution.py:300
  126.9 1.6 collective-permute-done.19.refs_6_
  128.5 0.9 collective-permute-start.21
  129.3 1.2 collective-permute-start.20
  130.5 14.1 %collective-permute-done.21.refs_9_ = bf16[432,672]{1,0:T(8,128)(2,1)S(1)} collective-permute-done((bf16[432,672]{1,0:T(8,128)(2,1)S(1)}, bf16[432,672]{1,0:T(8,128)(2,1)S(1)}, u32[]{:S(2)}, u32[]{:S(2)}) %collective-permute-start.21) | collective-permute-done | bytes 580640 | tf_op jit(solution)/shard_map/ppermute | solution.py:300
  144.7 3.8 %collective-permute-start.23 = (bf16[288,672]{1,0:T(8,128)(2,1)S(1)}, bf16[288,672]{1,0:T(8,128)(2,1)S(1)}, u32[]{:S(2)}, u32[]{:S(2)}) collective-permute-start(bf16[288,672]{1,0:T(8,128)(2,1)S(1)} %pad_maximum_fusion.3), channel_id=1, source_target_pairs={{0,96},{1,97},{4,100},{5,101},{8,104},{9,105},{12,108},{13,109},{1... | collective-permute-start | bytes 1161224 | tf_op jit(solution)/shard_map/ppermute | solution.py:300
  148.5 0.3 collective-permute-done.20.refs_8_
  149.0 9.8 %collective-permute-done.23.refs_11_ = bf16[288,672]{1,0:T(8,128)(2,1)S(1)} collective-permute-done((bf16[288,672]{1,0:T(8,128)(2,1)S(1)}, bf16[288,672]{1,0:T(8,128)(2,1)S(1)}, u32[]{:S(2)}, u32[]{:S(2)}) %collective-permute-start.23) | collective-permute-done | bytes 387104 | tf_op jit(solution)/shard_map/ppermute | solution.py:300
  158.8 3.0 %collective-permute-done.22.refs_10_ = bf16[288,672]{1,0:T(8,128)(2,1)S(1)} collective-permute-done((bf16[288,672]{1,0:T(8,128)(2,1)S(1)}, bf16[288,672]{1,0:T(8,128)(2,1)S(1)}, u32[]{:S(2)}, u32[]{:S(2)}) %collective-permute-start.22) | collective-permute-done | bytes 387104 | tf_op jit(solution)/shard_map/ppermute | solution.py:300
  161.8 6.5 %shard_map.78 = bf16[16,48,672]{2,1,0:T(8,128)(2,1)} custom-call(s32[2]{0:T(128)S(1)} %copy-done.3, bf16[512,768]{1,0:T(8,128)(2,1)S(1)} %pad_maximum_fusion.refs_0_, bf16[512,768]{1,0:T(8,128)(2,1)S(1)} %collective-permute-done.9.refs_1_, bf16[512,768]{1,0:T(8,128)(2,1)S(1)} %collective-permute-done.10.refs_2_, bf16[512,768]{1,0:T(8,128)(2,1)} %copy-done.8, ...), custom_call_target="tpu_custom_call" | custom-call | tf_op jit(solution)/shard_map/pallas_call | solution.py:272
  168.3 7.6 %all-to-all-start.1 = ((bf16[16,48,672]{2,1,0:T(8,128)(2,1)}), bf16[16,48,672]{2,1,0:T(8,128)(2,1)S(1)}, u32[]{:S(2)}, u32[]{:S(2)}) async-start(bf16[16,48,672]{2,1,0:T(8,128)(2,1)} %shard_map.78), calls=%async_computation.1 | async-start | bytes 2359296 | tf_op jit(solution)/shard_map/all_to_all | solution.py:372
  176.0 29.6 %all-to-all-done.1 = bf16[16,48,672]{2,1,0:T(8,128)(2,1)S(1)} async-done(((bf16[16,48,672]{2,1,0:T(8,128)(2,1)}), bf16[16,48,672]{2,1,0:T(8,128)(2,1)S(1)}, u32[]{:S(2)}, u32[]{:S(2)}) %all-to-all-start.1) | async-done | bytes 1032224 | tf_op jit(solution)/shard_map/all_to_all | solution.py:372
  205.9 0.7 copy.9
  206.6 0.2 convert_reduce_fusion
  206.8 0.7 reshape.16
  (62 shorter events, 1.1 us)
Async XLA Ops:
  0.6 3.9 %copy-start.9 = (bf16[1,16,8,2688]{3,2,1,0:T(8,128)(2,1)S(1)}, bf16[1,16,8,2688]{3,2,1,0:T(8,128)(2,1)}, u32[]{:S(2)}) copy-start(bf16[1,16,8,2688]{3,2,1,0:T(8,128)(2,1)} %param.5) | copy-start | bytes 2064388
  2.1 17.3 %collective-permute-start = (bf16[128,2688]{1,0:T(8,128)(2,1)S(1)}, bf16[128,2688]{1,0:T(8,128)(2,1)S(1)}, u32[]{:S(2)}, u32[]{:S(2)}) collective-permute-start(bf16[128,2688]{1,0:T(8,128)(2,1)S(1)} %get-tuple-element.72), channel_id=1, source_target_pairs={{0,2},{1,3},{4,6},{5,7},{8,10},{9,11},{12,14},{13,15},{16,18},{17,... | collective-permute-start | bytes 2064392 | tf_op jit(solution)/shard_map/ppermute | solution.py:300
  3.8 15.4 %copy-start.11 = (f32[2688]{0:T(1024)S(1)}, f32[2688]{0:T(1024)}, u32[]{:S(2)}) copy-start(f32[2688]{0:T(1024)} %param.9) | copy-start | bytes 32260
  3.8 17.0 %collective-permute-start.1 = (bf16[128,2688]{1,0:T(8,128)(2,1)S(1)}, bf16[128,2688]{1,0:T(8,128)(2,1)}, u32[]{:S(2)}, u32[]{:S(2)}) collective-permute-start(bf16[128,2688]{1,0:T(8,128)(2,1)S(1)} %get-tuple-element.71), channel_id=1, source_target_pairs={{0,130},{1,131},{4,134},{5,135},{8,138},{9,139},{12,142},{13,143},... | collective-permute-start | bytes 2064392 | tf_op jit(solution)/shard_map/ppermute | solution.py:300
  5.6 36.0 %all-to-all-start = ((bf16[64,2,2688]{2,1,0:T(2,128)(2,1)}), bf16[64,2,2688]{2,1,0:T(2,128)(2,1)S(1)}, u32[]{:S(2)}, u32[]{:S(2)}) async-start(bf16[64,2,2688]{2,1,0:T(2,128)(2,1)} %reshape_squeeze.6), calls=%async_computation | async-start | bytes 1376256 | tf_op jit(solution)/shard_map/all_to_all | solution.py:339
  19.0 47.3 %collective-permute-start.12 = (bf16[672,2688]{1,0:T(8,128)(2,1)}, bf16[672,2688]{1,0:T(8,128)(2,1)}, u32[]{:S(2)}, u32[]{:S(2)}) collective-permute-start(bf16[672,2688]{1,0:T(8,128)(2,1)} %refs_0_.1), channel_id=1, source_target_pairs={{0,1},{1,0},{4,5},{5,4},{8,9},{9,8},{12,13},{13,12},{16,17},{17,16... | collective-permute-start | bytes 10838024 | tf_op jit(solution)/shard_map/ppermute | solution.py:300
  19.2 22.4 %copy-start.1 = (f32[1,2688]{1,0:T(1,128)}, f32[1,2688]{1,0:T(1,128)S(1)}, u32[]{:S(2)}) copy-start(f32[1,2688]{1,0:T(1,128)S(1)} %reshape.15.gain_ref.refs_13_) | copy-start | bytes 32260
  19.3 22.3 %copy-start.2 = (s32[2]{0:T(128)}, s32[2]{0:T(128)S(1)}, u32[]{:S(2)}) copy-start(s32[2]{0:T(128)S(1)} %pad_add_fusion.place_ref) | copy-start | bytes 28
  19.3 22.3 %copy-start.4 = (bf16[16,8,2688]{2,1,0:T(8,128)(2,1)S(1)}, bf16[16,8,2688]{2,1,0:T(8,128)(2,1)}, u32[]{:S(2)}) copy-start(bf16[16,8,2688]{2,1,0:T(8,128)(2,1)} %inject_ref.1) | copy-start | bytes 2064388
  19.4 36.4 %copy-start.14 = (bf16[128,2688]{1,0:T(8,128)(2,1)}, bf16[128,2688]{1,0:T(8,128)(2,1)S(1)}, u32[]{:S(2)}) copy-start(bf16[128,2688]{1,0:T(8,128)(2,1)S(1)} %collective-permute-done.refs_2_) | copy-start | bytes 2064388
  23.6 38.1 %collective-permute-start.2 = (bf16[208,2688]{1,0:T(8,128)(2,1)}, bf16[208,2688]{1,0:T(8,128)(2,1)}, u32[]{:S(2)}, u32[]{:S(2)}) collective-permute-start(bf16[208,2688]{1,0:T(8,128)(2,1)} %get-tuple-element.70), channel_id=1, source_target_pairs={{0,2},{1,3},{4,6},{5,7},{8,10},{9,11},{12,14},{13,15},{16,18},{17,... | collective-permute-start | bytes 3354632 | tf_op jit(solution)/shard_map/ppermute | solution.py:300
  25.0 36.7 %collective-permute-start.3 = (bf16[208,2688]{1,0:T(8,128)(2,1)S(1)}, bf16[208,2688]{1,0:T(8,128)(2,1)}, u32[]{:S(2)}, u32[]{:S(2)}) collective-permute-start(bf16[208,2688]{1,0:T(8,128)(2,1)S(1)} %get-tuple-element.69), channel_id=1, source_target_pairs={{0,130},{1,131},{4,134},{5,135},{8,138},{9,139},{12,142},{13,143},... | collective-permute-start | bytes 3354632 | tf_op jit(solution)/shard_map/ppermute | solution.py:300
  44.7 0.9 copy-start.6
  45.6 18.4 %copy-start.5 = (f32[128,2688]{1,0:T(8,128)}, f32[128,2688]{1,0:T(8,128)S(1)}, u32[]{:S(2)}) copy-start(f32[128,2688]{1,0:T(8,128)S(1)} %get-tuple-element.49.refs_11_) | copy-start | bytes 4128772
  45.6 19.1 %copy-start.7 = (f32[128,128]{1,0:T(8,128)}, f32[128,128]{1,0:T(8,128)S(1)}, u32[]{:S(2)}) copy-start(f32[128,128]{1,0:T(8,128)S(1)} %get-tuple-element.50.refs_12_) | copy-start | bytes 196612
  45.6 8.0 %collective-permute-start.6 = (bf16[128,768]{1,0:T(8,128)(2,1)S(1)}, bf16[128,768]{1,0:T(8,128)(2,1)S(1)}, u32[]{:S(2)}, u32[]{:S(2)}) collective-permute-start(bf16[128,768]{1,0:T(8,128)(2,1)S(1)} %get-tuple-element.40), channel_id=1, source_target_pairs={{0,32},{1,33},{4,36},{5,37},{8,40},{9,41},{12,44},{13,45},{16,48},... | collective-permute-start | bytes 589832 | tf_op jit(solution)/shard_map/ppermute | solution.py:300
  45.6 10.1 %collective-permute-start.7 = (bf16[128,768]{1,0:T(8,128)(2,1)S(1)}, bf16[128,768]{1,0:T(8,128)(2,1)S(1)}, u32[]{:S(2)}, u32[]{:S(2)}) collective-permute-start(bf16[128,768]{1,0:T(8,128)(2,1)S(1)} %get-tuple-element.41), channel_id=1, source_target_pairs={{0,64},{1,65},{4,68},{5,69},{8,72},{9,73},{12,76},{13,77},{16,80},... | collective-permute-start | bytes 589832 | tf_op jit(solution)/shard_map/ppermute | solution.py:300
  53.7 5.7 %collective-permute-start.8 = (bf16[128,768]{1,0:T(8,128)(2,1)S(1)}, bf16[128,768]{1,0:T(8,128)(2,1)S(1)}, u32[]{:S(2)}, u32[]{:S(2)}) collective-permute-start(bf16[128,768]{1,0:T(8,128)(2,1)S(1)} %get-tuple-element.42), channel_id=1, source_target_pairs={{0,96},{1,97},{4,100},{5,101},{8,104},{9,105},{12,108},{13,109},{1... | collective-permute-start | bytes 589832 | tf_op jit(solution)/shard_map/ppermute | solution.py:300
  55.8 3.6 %collective-permute-start.4 = (bf16[128,2688]{1,0:T(8,128)(2,1)S(1)}, bf16[128,2688]{1,0:T(8,128)(2,1)S(1)}, u32[]{:S(2)}, u32[]{:S(2)}) collective-permute-start(bf16[128,2688]{1,0:T(8,128)(2,1)S(1)} %collective-permute-done.refs_2_), channel_id=1, source_target_pairs={{0,1},{1,0},{4,5},{5,4},{8,9},{9,8},{12,13},{13,12},{16,17},{17,16... | collective-permute-start | bytes 2064392 | tf_op jit(solution)/shard_map/ppermute | solution.py:300
  59.3 2.4 %collective-permute-start.5 = (bf16[128,2688]{1,0:T(8,128)(2,1)}, bf16[128,2688]{1,0:T(8,128)(2,1)S(1)}, u32[]{:S(2)}, u32[]{:S(2)}) collective-permute-start(bf16[128,2688]{1,0:T(8,128)(2,1)} %collective-permute-done.1.refs_4_), channel_id=1, source_target_pairs={{0,1},{1,0},{4,5},{5,4},{8,9},{9,8},{12,13},{13,12},{16,17},{17,16... | collective-permute-start | bytes 2064392 | tf_op jit(solution)/shard_map/ppermute | solution.py:300
  59.4 7.0 %copy-start.15 = (bf16[128,2688]{1,0:T(8,128)(2,1)}, bf16[128,2688]{1,0:T(8,128)(2,1)S(1)}, u32[]{:S(2)}) copy-start(bf16[128,2688]{1,0:T(8,128)(2,1)S(1)} %collective-permute-done.4.refs_3_) | copy-start | bytes 2064388
  61.7 0.9 copy-start.16
  61.7 3.1 %collective-permute-start.13 = (bf16[208,2688]{1,0:T(8,128)(2,1)}, bf16[208,2688]{1,0:T(8,128)(2,1)S(1)}, u32[]{:S(2)}, u32[]{:S(2)}) collective-permute-start(bf16[208,2688]{1,0:T(8,128)(2,1)} %collective-permute-done.2.refs_6_), channel_id=1, source_target_pairs={{0,1},{1,0},{4,5},{5,4},{8,9},{9,8},{12,13},{13,12},{16,17},{17,16... | collective-permute-start | bytes 3354632 | tf_op jit(solution)/shard_map/ppermute | solution.py:300
  61.9 4.4 %collective-permute-start.14 = (bf16[208,2688]{1,0:T(8,128)(2,1)}, bf16[208,2688]{1,0:T(8,128)(2,1)S(1)}, u32[]{:S(2)}, u32[]{:S(2)}) collective-permute-start(bf16[208,2688]{1,0:T(8,128)(2,1)} %collective-permute-done.3.refs_8_), channel_id=1, source_target_pairs={{0,1},{1,0},{4,5},{5,4},{8,9},{9,8},{12,13},{13,12},{16,17},{17,16... | collective-permute-start | bytes 3354632 | tf_op jit(solution)/shard_map/ppermute | solution.py:300
  62.6 51.8 %collective-permute-start.10 = (bf16[512,768]{1,0:T(8,128)(2,1)S(1)}, bf16[512,768]{1,0:T(8,128)(2,1)S(1)}, u32[]{:S(2)}, u32[]{:S(2)}) collective-permute-start(bf16[512,768]{1,0:T(8,128)(2,1)S(1)} %pad_maximum_fusion.refs_0_), channel_id=1, source_target_pairs={{0,2},{1,3},{4,6},{5,7},{8,10},{9,11},{12,14},{13,15},{16,18},{17,... | collective-permute-start | bytes 2359304 | tf_op jit(solution)/shard_map/ppermute | solution.py:300
  63.9 50.4 %collective-permute-start.11 = (bf16[512,768]{1,0:T(8,128)(2,1)S(1)}, bf16[512,768]{1,0:T(8,128)(2,1)S(1)}, u32[]{:S(2)}, u32[]{:S(2)}) collective-permute-start(bf16[512,768]{1,0:T(8,128)(2,1)S(1)} %pad_maximum_fusion.refs_0_), channel_id=1, source_target_pairs={{0,3},{1,2},{4,7},{5,6},{8,11},{9,10},{12,15},{13,14},{16,19},{17,... | collective-permute-start | bytes 2359304 | tf_op jit(solution)/shard_map/ppermute | solution.py:300
  64.8 1.6 copy-start.12
  64.8 49.6 %collective-permute-start.9 = (bf16[512,768]{1,0:T(8,128)(2,1)S(1)}, bf16[512,768]{1,0:T(8,128)(2,1)S(1)}, u32[]{:S(2)}, u32[]{:S(2)}) collective-permute-start(bf16[512,768]{1,0:T(8,128)(2,1)S(1)} %pad_maximum_fusion.refs_0_), channel_id=1, source_target_pairs={{0,1},{1,0},{4,5},{5,4},{8,9},{9,8},{12,13},{13,12},{16,17},{17,16... | collective-permute-start | bytes 2359304 | tf_op jit(solution)/shard_map/ppermute | solution.py:300
  66.4 1.0 copy-start.13
  114.3 30.4 %copy-start.8 = (bf16[512,768]{1,0:T(8,128)(2,1)}, bf16[512,768]{1,0:T(8,128)(2,1)S(1)}, u32[]{:S(2)}) copy-start(bf16[512,768]{1,0:T(8,128)(2,1)S(1)} %collective-permute-done.11.refs_3_) | copy-start | bytes 2359300
  114.4 2.0 collective-permute-start.15
  114.5 8.5 %collective-permute-start.16 = (bf16[144,672]{1,0:T(8,128)(2,1)}, bf16[144,672]{1,0:T(8,128)(2,1)S(1)}, u32[]{:S(2)}, u32[]{:S(2)}) collective-permute-start(bf16[144,672]{1,0:T(8,128)(2,1)} %get-tuple-element.62), channel_id=1, source_target_pairs={{0,2},{1,3},{4,6},{5,7},{8,10},{9,11},{12,14},{13,15},{16,18},{17,... | collective-permute-start | bytes 580616 | tf_op jit(solution)/shard_map/ppermute | solution.py:300
  116.0 10.8 %collective-permute-start.17 = (bf16[144,672]{1,0:T(8,128)(2,1)}, bf16[144,672]{1,0:T(8,128)(2,1)S(1)}, u32[]{:S(2)}, u32[]{:S(2)}) collective-permute-start(bf16[144,672]{1,0:T(8,128)(2,1)} %get-tuple-element.63), channel_id=1, source_target_pairs={{0,3},{1,2},{4,7},{5,6},{8,11},{9,10},{12,15},{13,14},{16,19},{17,... | collective-permute-start | bytes 580616 | tf_op jit(solution)/shard_map/ppermute | solution.py:300
  116.3 10.5 %collective-permute-start.18 = (bf16[144,672]{1,0:T(8,128)(2,1)}, bf16[144,672]{1,0:T(8,128)(2,1)S(1)}, u32[]{:S(2)}, u32[]{:S(2)}) collective-permute-start(bf16[144,672]{1,0:T(8,128)(2,1)} %get-tuple-element.65.refs_4_), channel_id=1, source_target_pairs={{0,32},{1,33},{4,36},{5,37},{8,40},{9,41},{12,44},{13,45},{16,48},... | collective-permute-start | bytes 580616 | tf_op jit(solution)/shard_map/ppermute | solution.py:300
  117.8 10.6 %collective-permute-start.19 = (bf16[144,672]{1,0:T(8,128)(2,1)}, bf16[144,672]{1,0:T(8,128)(2,1)S(1)}, u32[]{:S(2)}, u32[]{:S(2)}) collective-permute-start(bf16[144,672]{1,0:T(8,128)(2,1)} %get-tuple-element.65.refs_4_), channel_id=1, source_target_pairs={{0,96},{1,97},{4,100},{5,101},{8,104},{9,105},{12,108},{13,109},{1... | collective-permute-start | bytes 580616 | tf_op jit(solution)/shard_map/ppermute | solution.py:300
  128.5 16.1 %collective-permute-start.21 = (bf16[432,672]{1,0:T(8,128)(2,1)S(1)}, bf16[432,672]{1,0:T(8,128)(2,1)S(1)}, u32[]{:S(2)}, u32[]{:S(2)}) collective-permute-start(bf16[432,672]{1,0:T(8,128)(2,1)S(1)} %pad_maximum_fusion.1.refs_7_), channel_id=1, source_target_pairs={{0,96},{1,97},{4,100},{5,101},{8,104},{9,105},{12,108},{13,109},{1... | collective-permute-start | bytes 1741832 | tf_op jit(solution)/shard_map/ppermute | solution.py:300
  129.3 19.5 %collective-permute-start.20 = (bf16[432,672]{1,0:T(8,128)(2,1)S(1)}, bf16[432,672]{1,0:T(8,128)(2,1)S(1)}, u32[]{:S(2)}, u32[]{:S(2)}) collective-permute-start(bf16[432,672]{1,0:T(8,128)(2,1)S(1)} %pad_maximum_fusion.1.refs_7_), channel_id=1, source_target_pairs={{0,32},{1,33},{4,36},{5,37},{8,40},{9,41},{12,44},{13,45},{16,48},... | collective-permute-start | bytes 1741832 | tf_op jit(solution)/shard_map/ppermute | solution.py:300
  144.6 17.2 %copy-start = (bf16[144,672]{1,0:T(8,128)(2,1)S(1)}, bf16[144,672]{1,0:T(8,128)(2,1)}, u32[]{:S(2)}) copy-start(bf16[144,672]{1,0:T(8,128)(2,1)} %get-tuple-element.65.refs_4_) | copy-start | bytes 580612
  144.6 17.1 %copy-start.3 = (s32[2]{0:T(128)S(1)}, s32[2]{0:T(128)}, u32[]{:S(2)}) copy-start(s32[2]{0:T(128)} %copy-done.2) | copy-start | bytes 28
  144.7 14.0 %collective-permute-start.23 = (bf16[288,672]{1,0:T(8,128)(2,1)S(1)}, bf16[288,672]{1,0:T(8,128)(2,1)S(1)}, u32[]{:S(2)}, u32[]{:S(2)}) collective-permute-start(bf16[288,672]{1,0:T(8,128)(2,1)S(1)} %pad_maximum_fusion.3), channel_id=1, source_target_pairs={{0,96},{1,97},{4,100},{5,101},{8,104},{9,105},{12,108},{13,109},{1... | collective-permute-start | bytes 1161224 | tf_op jit(solution)/shard_map/ppermute | solution.py:300
  148.9 12.9 %collective-permute-start.22 = (bf16[288,672]{1,0:T(8,128)(2,1)S(1)}, bf16[288,672]{1,0:T(8,128)(2,1)S(1)}, u32[]{:S(2)}, u32[]{:S(2)}) collective-permute-start(bf16[288,672]{1,0:T(8,128)(2,1)S(1)} %pad_maximum_fusion.2), channel_id=1, source_target_pairs={{0,32},{1,33},{4,36},{5,37},{8,40},{9,41},{12,44},{13,45},{16,48},... | collective-permute-start | bytes 1161224 | tf_op jit(solution)/shard_map/ppermute | solution.py:300
  168.3 37.3 %all-to-all-start.1 = ((bf16[16,48,672]{2,1,0:T(8,128)(2,1)}), bf16[16,48,672]{2,1,0:T(8,128)(2,1)S(1)}, u32[]{:S(2)}, u32[]{:S(2)}) async-start(bf16[16,48,672]{2,1,0:T(8,128)(2,1)} %shard_map.78), calls=%async_computation.1 | async-start | bytes 2359296 | tf_op jit(solution)/shard_map/all_to_all | solution.py:372
  206.7 0.7 copy-start.10
